TPU v7x, 32 devices: a whole 2x2x4 slice. The times are simulated.
32 devices in a mesh: row: 16 (over z, y, x), col: 2 (over core).
Axes of the slice: x: 2, y: 2, z: 4, core: 2. Of those that a mesh axis runs over, the one named last changes fastest.
Arguments:
- near_blocks: float32 [128, 2, 256, 256], P('row', 'col'), may hold values from -0.25 to 0.25
- column_block: int32 [128, 2], P('row', 'col'), may hold values from 0 to 127, as said below
- test_panels: float32 [128, 256, 256], P(('row', 'col')), may hold values from -6 to 6
- nugget: float32 [128, 256], P('row'), may hold values from 0.5 to 2
Outputs:
- leaf_basis: float32 [128, 128, 256], P('row', None, 'col')
- leaf_miss: float32 [128, 128, 256], P('row', None, 'col')
- local_basis: float32 [112, 128, 256], P('row', None, 'col')
- upper_basis: float32 [16, 128, 256], P('row', None, 'col')
Inputs may be any that keep to these rules, and one draw needn't show every extreme that they name: `column_block`: row i names 2 different leaf blocks, i itself among them, all within i - 8 to i + 8.
All inputs are finite; a program needn't handle non-finite values.
Results may differ from a plain program's by a relative error of at most 0.0003.
Values sent between devices are 32-bit elements; how exact they have to be, the bound alone decides.
A program may use at most 64 MiB of HBM per device.

v0:
```python
import math

import jax
import jax.numpy as jnp
from jax import lax
from jax.sharding import PartitionSpec as P


def padded(block, sides, width):
    for axis, dim in sides:
        count = lax.axis_size(axis)
        forward = [(i, i + 1) for i in range(count - 1)]
        backward = [(target, source) for source, target in forward]
        low = lax.ppermute(
            lax.slice_in_dim(block, block.shape[dim] - width, None, axis=dim), axis, forward
        )
        high = lax.ppermute(lax.slice_in_dim(block, 0, width, axis=dim), axis, backward)
        block = jnp.concatenate([low, block, high], axis=dim)
    return block


def from_partner(block, axis, stride):
    count = lax.axis_size(axis)
    route = []
    for low in range(count):
        high = low | 1 << stride
        if high != low and high < count:
            route += [(low, high), (high, low)]
    return lax.ppermute(block, axis, route)


def product(left, right):
    return jnp.matmul(left, right, precision=lax.Precision.HIGHEST)


def combine(factor_a, panel_a, factor_b, panel_b):
    gram_matrix = product(factor_a, jnp.swapaxes(factor_a, -1, -2)) + product(
        factor_b, jnp.swapaxes(factor_b, -1, -2)
    )
    factor = jnp.linalg.cholesky(gram_matrix)
    basis_node = jax.scipy.linalg.solve_triangular(
        factor, jnp.concatenate([factor_a, factor_b], axis=-1), lower=True
    )
    reduced = jax.scipy.linalg.solve_triangular(
        factor, product(factor_a, panel_a) + product(factor_b, panel_b), lower=True
    )
    return (basis_node, factor, reduced)


def leaf_factor(panel_one, panel_two, gram_matrix, cross_gram):
    factor = jnp.linalg.cholesky(gram_matrix)
    basis_leaf = jax.scipy.linalg.solve_triangular(factor, panel_one, lower=True)
    reduced = jax.scipy.linalg.solve_triangular(factor, cross_gram, lower=True)
    missed = panel_two - jnp.einsum(
        "ist,isa->ita", reduced, basis_leaf, precision=lax.Precision.HIGHEST
    )
    return (basis_leaf, missed, factor, reduced)


def on_device(near_blocks, column_block, test_panels, nugget):
    leaf_count = near_blocks.shape[0]
    block_size = near_blocks.shape[2]
    panel_width = test_panels.shape[2] // 2
    piece_leaves = test_panels.shape[0]
    row_index = lax.axis_index("row")
    column_index = lax.axis_index("col")
    column_count = lax.axis_size("col")
    offsets = column_block - (row_index * leaf_count - leaf_count)
    own_within = jnp.arange(leaf_count, dtype=jnp.int32)
    edged_test = padded(test_panels, (("row", 0),), piece_leaves)
    widened = lax.all_gather(edged_test, "col", axis=0, tiled=True)
    margin_part = offsets // leaf_count
    within = offsets % leaf_count
    positions = (
        within // piece_leaves * (3 * piece_leaves)
        + margin_part * piece_leaves
        + within % piece_leaves
    )
    own_slots = (
        own_within // piece_leaves * (3 * piece_leaves) + piece_leaves + own_within % piece_leaves
    )
    picked = jnp.take(widened, positions, axis=0)
    partial_value = jnp.einsum(
        "ikab,ikbs->isa", near_blocks, picked, precision=lax.Precision.HIGHEST
    )
    own_rows = jnp.take(widened, own_slots, axis=0)
    sample = lax.psum(partial_value, "col") + jnp.swapaxes(own_rows, 1, 2) * nugget[:, None, :]
    panel_one = sample[:, :panel_width]
    panel_two = sample[:, panel_width:]
    gram_matrix = jnp.einsum("isa,ita->ist", panel_one, panel_one, precision=lax.Precision.HIGHEST)
    cross_gram = jnp.einsum("isa,ita->ist", panel_one, panel_two, precision=lax.Precision.HIGHEST)
    basis_leaf, missed, factor, reduced = leaf_factor(panel_one, panel_two, gram_matrix, cross_gram)
    row_share = block_size // column_count
    leaf_basis = lax.dynamic_slice_in_dim(basis_leaf, column_index * row_share, row_share, 2)
    leaf_miss = lax.dynamic_slice_in_dim(missed, column_index * row_share, row_share, 2)
    current_factor, current_panel = (factor, reduced)
    local_parts = []
    for level_index in range(leaf_count.bit_length() - 1):
        pair_count = current_factor.shape[0] // 2
        pair_factor = current_factor.reshape(pair_count, 2, panel_width, panel_width)
        pair_panel = current_panel.reshape(pair_count, 2, panel_width, panel_width)
        basis_level, current_factor, current_panel = combine(
            pair_factor[:, 0], pair_panel[:, 0], pair_factor[:, 1], pair_panel[:, 1]
        )
        local_parts.append(basis_level)
    local_basis = jnp.concatenate(local_parts, axis=0)
    factor_top = current_factor[0]
    panel_top = current_panel[0]
    levels = lax.axis_size("row").bit_length() - 1
    upper_basis = jnp.zeros((panel_width, 2 * panel_width), jnp.float32)
    for level_index in range(levels):
        stride = 1 << level_index
        partner_factor, partner_panel = from_partner((factor_top, panel_top), "row", level_index)
        upper_side = row_index // stride % 2 == 1
        left_factor = jnp.where(upper_side, partner_factor, factor_top)
        left_panel = jnp.where(upper_side, partner_panel, panel_top)
        right_factor = jnp.where(upper_side, factor_top, partner_factor)
        right_panel = jnp.where(upper_side, panel_top, partner_panel)
        basis_node, factor_top, panel_top = combine(
            left_factor, left_panel, right_factor, right_panel
        )
        upper_basis = jnp.where(row_index % (2 * stride) == stride, basis_node, upper_basis)
    root_scale = 1.0 / math.sqrt(leaf_count * lax.axis_size("row") * block_size)
    root_stack = jnp.concatenate([jnp.swapaxes(factor_top, 0, 1), panel_top], axis=1) * root_scale
    upper_basis = jnp.where(row_index == 0, root_stack, upper_basis)
    column_share = 2 * panel_width // column_count
    local_share = lax.dynamic_slice_in_dim(
        local_basis, column_index * column_share, column_share, 2
    )
    upper_share = lax.dynamic_slice_in_dim(
        upper_basis, column_index * column_share, column_share, 1
    )
    return (leaf_basis, leaf_miss, local_share, upper_share[None])


def solution(mesh):
    placed = (
        P("row", "col", None, None),
        P("row", "col"),
        P(("row", "col"), None, None),
        P("row", None),
    )
    return jax.shard_map(
        on_device,
        mesh=mesh,
        in_specs=placed,
        out_specs=(
            P("row", None, "col"),
            P("row", None, "col"),
            P("row", None, "col"),
            P("row", None, "col"),
        ),
        check_vma=False,
    )
```

profile of v0, /device:TPU:0, one launch (start us, length us, event | category | flops | bytes accessed | tf_op | source)
XLA Modules:
  0.0 612.3 jit_solution(12506938654470618584)
XLA Ops:
  7.2 5.0 collective-permute-start
  12.3 1.3 collective-permute-start.1
  13.6 43.8 %collective-permute-done = f32[4,256,256]{2,1,0:T(8,128)S(1)} collective-permute-done((f32[4,256,256]{2,1,0:T(8,128)}, f32[4,256,256]{2,1,0:T(8,128)S(1)}, u32[]{:S(2)}, u32[]{:S(2)}) %collective-permute-start) | collective-permute-done | bytes 1048608 | tf_op jit(solution)/shard_map/ppermute | solution.py:14
  57.4 1.8 collective-permute-done.1
  59.2 3.1 pad_maximum_fusion
  63.1 16.5 %all-gather.2.cloned.1.call-done = f32[24,256,256]{2,1,0:T(8,128)} async-done(((f32[12,256,256]{2,1,0:T(8,128)}), f32[24,256,256]{2,1,0:T(8,128)}) %all-gather.2.cloned.1.call-update) | async-done | bytes 6291472 | tf_op jit(solution)/shard_map/all_gather | solution.py:71
  79.6 4.8 gather_fusion
  84.4 3.0 copy.129
  87.4 5.1 fusion
  92.7 4.8 gather_fusion.1
  97.4 3.0 copy.130
  100.4 14.6 %all-reduce.2.cloned.1.call-done = f32[8,256,256]{2,1,0:T(8,128)} async-done(((f32[8,256,256]{2,1,0:T(8,128)}), f32[8,256,256]{2,1,0:T(8,128)}) %all-reduce.2.cloned.1.call-update) | async-done | bytes 2097168 | tf_op jit(solution)/shard_map/psum | solution.py:87
  115.0 2.6 bitcast_add_fusion
  117.6 1.1 fusion.9
  118.9 1.9 fusion.5
  121.0 0.9 fusion.18
  121.9 94.6 %custom-call.45 = f32[8,128,128]{2,1,0:T(8,128)S(1)} custom-call(f32[8,128,128]{2,1,0:T(8,128)} %fusion.18), custom_call_target="Cholesky" | custom-call | tf_op jit(solution)/shard_map/jit(cholesky)/cholesky | solution.py:51
  216.6 0.9 select_bitcast_fusion
  219.1 47.1 %custom-call.47 = f32[4,128,128]{2,1,0:T(8,128)S(1)} custom-call(f32[4,128,128]{2,1,0:T(8,128)S(1)} %fusion.29), custom_call_target="Cholesky" | custom-call | tf_op jit(solution)/shard_map/jit(cholesky)/cholesky | solution.py:40
  266.4 0.8 select_bitcast_fusion.1
  268.1 23.8 %custom-call.49 = f32[2,128,128]{2,1,0:T(8,128)S(1)} custom-call(f32[2,128,128]{2,1,0:T(8,128)S(1)} %fusion.51), custom_call_target="Cholesky" | custom-call | tf_op jit(solution)/shard_map/jit(cholesky)/cholesky | solution.py:40
  292.1 0.7 fusion.52
  294.5 0.8 slice_bitcast_fusion.5
  295.3 0.9 convolution_add_fusion.13
  296.2 1.6 copy.149
  297.8 1.5 fusion.57
  299.3 13.2 %custom-call.51 = f32[1,128,128]{2,1,0:T(8,128)} custom-call(f32[1,128,128]{2,1,0:T(8,128)} %fusion.57), custom_call_target="Cholesky" | custom-call | tf_op jit(solution)/shard_map/jit(cholesky)/cholesky | solution.py:40
  312.4 0.9 select_reduce_fusion.7
  313.9 2.1 select_bitcast_fusion.7
  316.0 1.7 collective-permute-start.2
  317.7 80.0 %custom-call.46 = f32[8,1,128,128]{2,3,1,0:T(8,128)} custom-call(f32[8,1,128,128]{3,2,1,0:T(8,128)} %get-tuple-element.17), custom_call_target="InvertDiagBlocksLowerTriangular" | custom-call | tf_op jit(solution)/shard_map/jit(_solve_triangular)/vmap()/triangular_solve | solution.py:52
  397.7 3.5 fusion.7
  401.2 1.0 fusion.15
  402.6 1.1 convolution_add_fusion
  403.8 40.8 %custom-call.48 = f32[4,1,128,128]{2,3,1,0:T(8,128)} custom-call(f32[4,1,128,128]{3,2,1,0:T(8,128)} %get-tuple-element.15), custom_call_target="InvertDiagBlocksLowerTriangular" | custom-call | tf_op jit(solution)/shard_map/jit(_solve_triangular)/vmap()/triangular_solve | solution.py:41
  444.6 1.6 fusion.26
  446.5 0.9 convolution_add_fusion.2
  447.4 20.7 %custom-call.50 = f32[2,1,128,128]{2,3,1,0:T(8,128)S(1)} custom-call(f32[2,1,128,128]{3,2,1,0:T(8,128)} %get-tuple-element.26), custom_call_target="InvertDiagBlocksLowerTriangular" | custom-call | tf_op jit(solution)/shard_map/jit(_solve_triangular)/vmap()/triangular_solve | solution.py:41
  468.7 1.3 convolution_bitcast_fusion
  470.3 0.8 convolution_add_fusion.8
  471.1 10.6 %custom-call.60 = f32[1,128,128]{1,2,0:T(8,128)S(1)} custom-call(f32[1,128,128]{2,1,0:T(8,128)} %get-tuple-element.13), custom_call_target="InvertDiagBlocksLowerTriangular" | custom-call | tf_op jit(solution)/shard_map/jit(_solve_triangular)/triangular_solve/custom-call.11 | solution.py:41
  481.8 1.2 fusion.77
  483.3 2.1 fusion.128
  485.4 1.2 convolution_bitcast_fusion.1
  486.6 1.4 fusion.22
  488.7 1.1 dynamic-slice_subtract_fusion
  489.8 0.8 fusion.20
  490.6 0.9 broadcast_select_fusion.1
  492.1 11.7 %cholesky.213 = f32[128,128]{1,0:T(8,128)S(1)} custom-call(f32[128,128]{1,0:T(8,128)S(1)} %fusion.76), custom_call_target="Cholesky" | custom-call | tf_op jit(solution)/shard_map/jit(cholesky)/cholesky | solution.py:40
  505.2 9.8 %custom-call.62 = f32[1,128,128]{1,2,0:T(8,128)S(1)} custom-call(f32[1,128,128]{2,1,0:T(8,128)S(1)} %get-tuple-element.11), custom_call_target="InvertDiagBlocksLowerTriangular" | custom-call | tf_op jit(solution)/shard_map/jit(_solve_triangular)/triangular_solve/custom-call.12 | solution.py:44
  515.6 1.8 collective-permute-start.3
  517.4 1.0 fusion.93
  520.5 11.7 %cholesky.224 = f32[128,128]{1,0:T(8,128)S(1)} custom-call(f32[128,128]{1,0:T(8,128)S(1)} %fusion.75), custom_call_target="Cholesky" | custom-call | tf_op jit(solution)/shard_map/jit(cholesky)/cholesky | solution.py:40
  533.6 9.8 %custom-call.63 = f32[1,128,128]{1,2,0:T(8,128)S(1)} custom-call(f32[1,128,128]{2,1,0:T(8,128)S(1)} %get-tuple-element.9), custom_call_target="InvertDiagBlocksLowerTriangular" | custom-call | tf_op jit(solution)/shard_map/jit(_solve_triangular)/triangular_solve/custom-call.12 | solution.py:44
  543.8 1.8 collective-permute-start.4
  546.7 2.0 collective-permute-done.4
  549.4 11.7 %cholesky.235 = f32[128,128]{1,0:T(8,128)S(1)} custom-call(f32[128,128]{1,0:T(8,128)S(1)} %fusion.74), custom_call_target="Cholesky" | custom-call | tf_op jit(solution)/shard_map/jit(cholesky)/cholesky | solution.py:40
  561.8 0.9 select_bitcast_fusion.4
  562.7 9.8 %custom-call.64 = f32[1,128,128]{1,2,0:T(8,128)S(1)} custom-call(f32[1,128,128]{2,1,0:T(8,128)S(1)} %get-tuple-element.7), custom_call_target="InvertDiagBlocksLowerTriangular" | custom-call | tf_op jit(solution)/shard_map/jit(_solve_triangular)/triangular_solve/custom-call.12 | solution.py:44
  572.9 2.5 collective-permute-start.5
  576.7 2.8 collective-permute-done.5
  580.2 11.7 %cholesky.246 = f32[128,128]{1,0:T(8,128)S(1)} custom-call(f32[128,128]{1,0:T(8,128)S(1)} %fusion.73), custom_call_target="Cholesky" | custom-call | tf_op jit(solution)/shard_map/jit(cholesky)/cholesky | solution.py:40
  593.3 9.8 %custom-call.65 = f32[1,128,128]{1,2,0:T(8,128)S(1)} custom-call(f32[1,128,128]{2,1,0:T(8,128)S(1)} %get-tuple-element.37), custom_call_target="InvertDiagBlocksLowerTriangular" | custom-call | tf_op jit(solution)/shard_map/jit(_solve_triangular)/triangular_solve/custom-call.12 | solution.py:44
  604.3 0.7 copy.172
  (118 shorter events, 22.4 us)
Async XLA Ops:
  7.2 80.2 %copy-start = (f32[8,1,256,256]{3,2,1,0:T(8,128)S(1)}, f32[8,1,256,256]{3,2,1,0:T(8,128)}, u32[]{:S(2)}) copy-start(f32[8,1,256,256]{3,2,1,0:T(8,128)} %param.9) | copy-start | bytes 6291460
  7.2 72.4 %all-gather.2.cloned.1.call-start = ((), (), s32[]{:S(2)}) async-start(), calls=%async_computation | async-start | bytes 9437184 | tf_op jit(solution)/shard_map/all_gather | solution.py:71
  7.2 50.2 %collective-permute-start = (f32[4,256,256]{2,1,0:T(8,128)}, f32[4,256,256]{2,1,0:T(8,128)S(1)}, u32[]{:S(2)}, u32[]{:S(2)}) collective-permute-start(f32[4,256,256]{2,1,0:T(8,128)} %param.11), channel_id=1, source_target_pairs={{0,2},{2,4},{4,6},{6,8},{8,10},{10,12},{12,14},{14,16},{16,18},{18... | collective-permute-start | bytes 3145736 | tf_op jit(solution)/shard_map/ppermute | solution.py:14
  12.3 47.0 %collective-permute-start.1 = (f32[4,256,256]{2,1,0:T(8,128)}, f32[4,256,256]{2,1,0:T(8,128)S(1)}, u32[]{:S(2)}, u32[]{:S(2)}) collective-permute-start(f32[4,256,256]{2,1,0:T(8,128)} %param.11), channel_id=1, source_target_pairs={{2,0},{4,2},{6,4},{8,6},{10,8},{12,10},{14,12},{16,14},{18,16},{20... | collective-permute-start | bytes 3145736 | tf_op jit(solution)/shard_map/ppermute | solution.py:17
  62.4 0.7 copy-start.12
  62.4 52.6 %all-reduce.2.cloned.1.call-start = ((), (), s32[]{:S(2)}) async-start(), calls=%async_computation.1 | async-start | bytes 4194304 | tf_op jit(solution)/shard_map/psum | solution.py:87
  97.4 17.6 %copy-start.11 = (f32[8,256]{1,0:T(8,128)S(1)}, f32[8,256]{1,0:T(8,128)}, u32[]{:S(2)}) copy-start(f32[8,256]{1,0:T(8,128)} %param.12) | copy-start | bytes 24580
  117.6 1.4 copy-start.1
  295.3 105.9 %copy-start.4 = (f32[8,128,128]{2,1,0:T(8,128)S(1)}, f32[8,128,128]{2,1,0:T(8,128)}, u32[]{:S(2)}) copy-start(f32[8,128,128]{2,1,0:T(8,128)} %fusion.5) | copy-start | bytes 1572868
  316.0 174.6 %collective-permute-start.2 = (f32[128,128]{1,0:T(8,128)}, f32[128,128]{1,0:T(8,128)}, u32[]{:S(2)}, u32[]{:S(2)}) collective-permute-start(f32[128,128]{1,0:T(8,128)} %get-tuple-element.14), channel_id=1, source_target_pairs={{0,2},{2,0},{4,6},{6,4},{8,10},{10,8},{12,14},{14,12},{16,18},{18,... | collective-permute-start | bytes 196616 | tf_op jit(solution)/shard_map/ppermute | solution.py:29
  397.7 3.5 copy-start.5
  402.2 1.5 copy-start.3
  403.8 79.6 %copy-start.2 = (f32[8,128,256]{2,1,0:T(8,128)S(1)}, f32[8,128,256]{2,1,0:T(8,128)}, u32[]{:S(2)}) copy-start(f32[8,128,256]{2,1,0:T(8,128)} %fusion.7) | copy-start | bytes 3145732
  468.1 0.6 copy-start.9
  470.0 18.0 %copy-start.6 = (f32[4,1,128,128]{2,3,1,0:T(8,128)S(1)}, f32[4,1,128,128]{2,3,1,0:T(8,128)}, u32[]{:S(2)}) copy-start(f32[4,1,128,128]{2,3,1,0:T(8,128)} %custom-call.48) | copy-start | bytes 786436
  481.7 4.9 copy-start.10
  481.7 6.3 %copy-start.7 = (f32[4,128,128]{2,1,0:T(8,128)S(1)}, f32[4,128,128]{2,1,0:T(8,128)}, u32[]{:S(2)}) copy-start(f32[4,128,128]{2,1,0:T(8,128)} %get-tuple-element.21) | copy-start | bytes 786436
  481.8 6.3 %copy-start.8 = (f32[4,128,128]{2,1,0:T(8,128)S(1)}, f32[4,128,128]{2,1,0:T(8,128)}, u32[]{:S(2)}) copy-start(f32[4,128,128]{2,1,0:T(8,128)} %get-tuple-element.22) | copy-start | bytes 786436
  483.0 5.7 slice-start
  483.0 34.4 %collective-permute-start.6 = (f32[128,128]{1,0:T(8,128)S(1)}, f32[128,128]{1,0:T(8,128)}, u32[]{:S(2)}, u32[]{:S(2)}) collective-permute-start(f32[128,128]{1,0:T(8,128)S(1)} %fusion.77), channel_id=1, source_target_pairs={{0,2},{2,0},{4,6},{6,4},{8,10},{10,8},{12,14},{14,12},{16,18},{18,... | collective-permute-start | bytes 196616 | tf_op jit(solution)/shard_map/ppermute | solution.py:29
  515.6 4.3 collective-permute-start.3
  518.9 26.7 %collective-permute-start.7 = (f32[128,128]{1,0:T(8,128)S(1)}, f32[128,128]{1,0:T(8,128)S(1)}, u32[]{:S(2)}, u32[]{:S(2)}) collective-permute-start(f32[128,128]{1,0:T(8,128)S(1)} %fusion.62), channel_id=1, source_target_pairs={{0,4},{4,0},{2,6},{6,2},{8,12},{12,8},{10,14},{14,10},{16,20},{20,... | collective-permute-start | bytes 196616 | tf_op jit(solution)/shard_map/ppermute | solution.py:29
  543.8 4.9 collective-permute-start.4
  546.3 29.0 %collective-permute-start.8 = (f32[128,128]{1,0:T(8,128)S(1)}, f32[128,128]{1,0:T(8,128)S(1)}, u32[]{:S(2)}, u32[]{:S(2)}) collective-permute-start(f32[128,128]{1,0:T(8,128)S(1)} %fusion.65), channel_id=1, source_target_pairs={{0,8},{8,0},{2,10},{10,2},{4,12},{12,4},{6,14},{14,6},{16,24},{24,... | collective-permute-start | bytes 196616 | tf_op jit(solution)/shard_map/ppermute | solution.py:29
  572.9 6.6 %collective-permute-start.5 = (f32[128,128]{1,0:T(8,128)S(1)}, f32[128,128]{1,0:T(8,128)S(1)}, u32[]{:S(2)}, u32[]{:S(2)}) collective-permute-start(f32[128,128]{1,0:T(8,128)S(1)} %get-tuple-element.8), channel_id=1, source_target_pairs={{0,16},{16,0},{2,18},{18,2},{4,20},{20,4},{6,22},{22,6},{8,24},{24... | collective-permute-start | bytes 196616 | tf_op jit(solution)/shard_map/ppermute | solution.py:29
  576.1 27.4 %collective-permute-start.9 = (f32[128,128]{1,0:T(8,128)S(1)}, f32[128,128]{1,0:T(8,128)S(1)}, u32[]{:S(2)}, u32[]{:S(2)}) collective-permute-start(f32[128,128]{1,0:T(8,128)S(1)} %fusion.68), channel_id=1, source_target_pairs={{0,16},{16,0},{2,18},{18,2},{4,20},{20,4},{6,22},{22,6},{8,24},{24... | collective-permute-start | bytes 196616 | tf_op jit(solution)/shard_map/ppermute | solution.py:29
Sparse Core Ops, SparseCore 0:
  62.5 17.0 all-gather.1
  92.6 22.3 all-reduce.1
where the time goes:
time: 622 us; the launch traced here: 612 us
  other arithmetic  440 us (71%)
  waiting for transfers between devices  82.3 us (13%)
  matrix products  36.5 us (6%)
  local copies, waits for them, and re-layouts  22.2 us (4%)
  starting transfers between devices  15.8 us (3%)
  between operations  15.3 us (2%)
    another operation x21, other arithmetic, combine(): factor = jnp.linalg.cholesky(gram_matrix)  135 us
    another operation x4, other arithmetic, leaf_factor(): factor = jnp.linalg.cholesky(gram_matrix)  94.7 us
    another operation x3, other arithmetic, leaf_factor(): jax.scipy.linalg.solve_triangular(factor, panel_one, lower=True)  81 us
    another operation x5, other arithmetic, combine(): jax.scipy.linalg.solve_triangular(factor, jnp.concatenate([factor_a, fact...  75 us
    ppermute x1, waiting for transfers between devices, padded(): lax.ppermute(lax.slice_in_dim(block, block.shape[dim] - width, None, axis...  43.8 us
    another operation x8, other arithmetic, combine(): jax.scipy.linalg.solve_triangular(factor, product(factor_a, panel_a) + pr...  42.1 us
    all_gather x1, waiting for transfers between devices, on_device(): widened = lax.all_gather(edged_test, 'col', axis=0, tiled=True)  16.5 us
    psum x1, waiting for transfers between devices, on_device(): lax.psum(partial_value, 'col')  14.6 us
  transfers between devices with their start and end apart: 12, of which 7 were waited for; matrix products, arithmetic and copies ran while one was open for 46% of the time, Pallas kernels for 0%

commit v1 on v0

v1 whole, which is shorter than its diff:
```python
import functools
import math

import jax
import jax.numpy as jnp
from jax import lax
from jax.experimental import pallas as pl
from jax.experimental.pallas import tpu as pltpu
from jax.sharding import PartitionSpec as P

STRIP = 32
SLAB = 8
LIMIT = 48 * 1024 * 1024


def dot(left, right, left_dim, right_dim):
    return lax.dot_general(
        left,
        right,
        (((left_dim,), (right_dim,)), ((), ())),
        precision=lax.Precision.HIGHEST,
        preferred_element_type=jnp.float32,
    )


def load_augmented(work, slot, gram):
    size = gram.shape[0]
    row = lax.broadcasted_iota(jnp.int32, (size, size), 0)
    lane = lax.broadcasted_iota(jnp.int32, (size, size), 1)
    work[slot, :, :size] = gram
    work[slot, :, size:] = jnp.where(row == lane, 1.0, 0.0)


def eliminate(work, first, count):
    size = work.shape[1]
    row = lax.broadcasted_iota(jnp.int32, (count, SLAB, 1), 1)
    lane = lax.broadcasted_iota(jnp.int32, (1, SLAB, 2 * size), 2)
    sub = lax.broadcasted_iota(jnp.int32, (1, SLAB, 2 * size), 1)
    own = pl.ds(first, count)
    for top in range(0, size, STRIP):
        slabs = [
            work[own, top + at : top + at + SLAB, :] for at in range(0, STRIP, SLAB)
        ]
        for step in range(STRIP):
            at, inner = divmod(step, SLAB)
            here = top + step
            column = slabs[at][:, :, here : here + 1]
            pivot_row = slabs[at][:, inner : inner + 1, :]
            pivot = column[:, inner : inner + 1, :]
            scaled = pivot_row * (1.0 / pivot)
            for later in range(at, len(slabs)):
                if later == at:
                    if inner == SLAB - 1:
                        continue
                    factor = jnp.where(row > inner, column, 0.0)
                else:
                    factor = slabs[later][:, :, here : here + 1]
                slabs[later] = slabs[later] - factor * scaled
        done = []
        for at, slab in enumerate(slabs):
            base = top + at * SLAB
            diagonal = jnp.sum(
                jnp.where(lane == sub + base, slab, 0.0), axis=2, keepdims=True
            )
            slab = slab * lax.rsqrt(diagonal)
            slab = jnp.where(lane >= sub + base, slab, 0.0)
            work[own, base : base + SLAB, :] = slab
        below = top + STRIP
        if below < size:
            for slot in range(first, first + count):
                strip = work[slot, top:below, :]
                work[slot, below:, :] -= dot(strip[:, below:size], strip, 0, 0)


def sample_kernel(place, near, panels, own, nugget, sample, moments, total):
    leaf, slot = pl.program_id(0), pl.program_id(1)
    width = moments.shape[1]
    part = dot(near[0, 0], panels[0], 1, 0)

    @pl.when(slot == 0)
    def _():
        sample[0] = part + own[0] * nugget[0]

    @pl.when(slot > 0)
    def _():
        sample[0] += part

    @pl.when(slot == pl.num_programs(1) - 1)
    def _():
        whole = sample[0]
        both = dot(whole[:, :width], whole, 0, 0)
        moments[0] = both

        @pl.when(leaf == 0)
        def _():
            total[...] = both

        @pl.when(leaf > 0)
        def _():
            total[...] += both


def sampled(near, place, panels, own_place, nugget):
    slots, leaves, block, _ = near.shape
    wide = panels.shape[2]
    width = wide // 2
    grid = pltpu.PrefetchScalarGridSpec(
        num_scalar_prefetch=1,
        grid=(leaves, slots),
        in_specs=[
            pl.BlockSpec((1, 1, block, block), lambda i, k, p: (k, i, 0, 0)),
            pl.BlockSpec((1, block, wide), lambda i, k, p: (p[i * (slots + 1) + k], 0, 0)),
            pl.BlockSpec((1, block, wide), lambda i, k, p: (p[i * (slots + 1) + slots], 0, 0)),
            pl.BlockSpec((1, block, 1), lambda i, k, p: (i, 0, 0)),
        ],
        out_specs=[
            pl.BlockSpec((1, block, wide), lambda i, k, p: (i, 0, 0)),
            pl.BlockSpec((1, width, wide), lambda i, k, p: (i, 0, 0)),
            pl.BlockSpec((width, wide), lambda i, k, p: (0, 0)),
        ],
    )
    index = jnp.concatenate([place.T, own_place[:, None]], axis=1).reshape(-1)
    return pl.pallas_call(
        sample_kernel,
        grid_spec=grid,
        out_shape=[
            jax.ShapeDtypeStruct((leaves, block, wide), jnp.float32),
            jax.ShapeDtypeStruct((leaves, width, wide), jnp.float32),
            jax.ShapeDtypeStruct((width, wide), jnp.float32),
        ],
        compiler_params=pltpu.CompilerParams(vmem_limit_bytes=LIMIT),
    )(index, near, panels, panels, nugget[:, :, None])


def local_kernel(columns, sample, moments, basis, missed, inner, work, sums):
    leaves, width, wide = moments.shape
    share = wide // columns
    column = lax.axis_index("col")
    side = column * share // width
    offset = pl.multiple_of(column * share % width, share)
    nodes = 2 * leaves - 1
    for leaf in range(leaves):
        sums[leaf] = moments[leaf, :, :width]
    for node in range(leaves, nodes):
        child = 2 * (node - leaves)
        sums[node] = sums[child] + sums[child + 1]
    for node in range(nodes):
        load_augmented(work, node, sums[node])
    eliminate(work, 0, nodes)
    points = pl.ds(pl.multiple_of(column * share, share), share)
    for leaf in range(leaves):
        inverse = work[leaf, :, width:]
        part = sample[leaf, points, :]
        own = dot(inverse, part[:, :width], 1, 1)
        basis[leaf] = own
        reduced = dot(inverse, moments[leaf, :, width:], 1, 0)
        missed[leaf] = part[:, width:].T - dot(reduced, own, 0, 0)
    for node in range(leaves, nodes):
        child = 2 * (node - leaves) + side
        inner[node - leaves] = dot(
            work[node, :, width:], work[child, pl.ds(offset, share), :width], 1, 1
        )


def upper_kernel(columns, scale, pair, root, upper, work):
    width, wide = root.shape[0], 2 * root.shape[0]
    share = wide // columns
    column = lax.axis_index("col")
    offset = pl.multiple_of(column * share % width, share)
    load_augmented(work, 0, pair[0])
    load_augmented(work, 1, pair[1])
    eliminate(work, 0, 2)
    inverse = work[0, :, width:]
    node = dot(inverse, work[1, pl.ds(offset, share), :width], 1, 1)
    top = dot(inverse, root[...], 1, 0) * scale
    upper[0] = jnp.where(lax.axis_index("row") == 0, top, node)


def whole_spec():
    return pl.BlockSpec(memory_space=pltpu.VMEM)


def local_bases(sample, moments, columns):
    leaves, width, wide = moments.shape
    share = wide // columns
    nodes = 2 * leaves - 1
    return pl.pallas_call(
        functools.partial(local_kernel, columns),
        in_specs=[whole_spec()] * 2,
        out_specs=[whole_spec()] * 3,
        out_shape=[
            jax.ShapeDtypeStruct((leaves, width, share), jnp.float32),
            jax.ShapeDtypeStruct((leaves, width, share), jnp.float32),
            jax.ShapeDtypeStruct((leaves - 1, width, share), jnp.float32),
        ],
        scratch_shapes=[
            pltpu.VMEM((nodes, width, wide), jnp.float32),
            pltpu.VMEM((nodes, width, width), jnp.float32),
        ],
        compiler_params=pltpu.CompilerParams(vmem_limit_bytes=LIMIT),
        cost_estimate=pl.CostEstimate(
            flops=10_000_000_000, bytes_accessed=4_000_000, transcendentals=0
        ),
    )(sample, moments)


def upper_bases(pair, root, columns, scale):
    width, wide = root.shape[0], 2 * root.shape[0]
    share = wide // columns
    return pl.pallas_call(
        functools.partial(upper_kernel, columns, scale),
        in_specs=[whole_spec()] * 2,
        out_specs=whole_spec(),
        out_shape=jax.ShapeDtypeStruct((1, width, share), jnp.float32),
        scratch_shapes=[pltpu.VMEM((2, width, wide), jnp.float32)],
        compiler_params=pltpu.CompilerParams(vmem_limit_bytes=LIMIT),
    )(pair, root)


def around(block, axis):
    count = lax.axis_size(axis)
    parts = [block]
    for shift in range(1, count):
        route = [((i + shift) % count, i) for i in range(count)]
        parts.append(lax.ppermute(block, axis, route))
    return parts


def on_device(near_blocks, column_block, test_panels, nugget):
    leaves = near_blocks.shape[0]
    block = near_blocks.shape[2]
    width = test_panels.shape[2] // 2
    piece = test_panels.shape[0]
    row = lax.axis_index("row")
    column = lax.axis_index("col")
    rows = lax.axis_size("row")
    columns = lax.axis_size("col")

    near = jnp.stack(around(near_blocks[:, 0], "col"))
    choice = jnp.stack(around(column_block[:, 0], "col"))
    forward = [(i, i + 1) for i in range(rows - 1)]
    backward = [(i + 1, i) for i in range(rows - 1)]
    low = lax.ppermute(test_panels, "row", forward)
    high = lax.ppermute(test_panels, "row", backward)
    panels = jnp.concatenate([low, test_panels, high], axis=0)
    panels = jnp.concatenate(around(panels, "col"), axis=0)

    def position(index):
        part, within = index // leaves, index % leaves
        shift = (within // piece - column + columns) % columns
        return shift * (3 * piece) + part * piece + within % piece

    place = position(choice - (row - 1) * leaves)
    own_place = position(jnp.arange(leaves, dtype=jnp.int32) + leaves)
    sample, moments, total = sampled(near, place, panels, own_place, nugget)

    basis, missed, inner = local_bases(sample, moments, columns)

    share = 2 * width // columns
    on_left = column * share // width == 0
    node, child = total[:, :width], total[:, :width]
    for level in range(rows.bit_length() - 1):
        stride = 1 << level
        route = [(i, i ^ stride) for i in range(rows)]
        other = lax.ppermute(total, "row", route)
        both = total + other
        here = row % (2 * stride) == stride
        node = jnp.where(here, both[:, :width], node)
        child = jnp.where(here, jnp.where(on_left, other, total)[:, :width], child)
        total = both
    node = jnp.where(row == 0, total[:, :width], node)
    root = lax.dynamic_slice_in_dim(total, column * share, share, 1)
    scale = 1.0 / math.sqrt(leaves * rows * block)
    upper = upper_bases(jnp.stack([node, child]), root, columns, scale)
    return (basis, missed, inner, upper)


def solution(mesh):
    placed = (
        P("row", "col", None, None),
        P("row", "col"),
        P(("row", "col"), None, None),
        P("row", None),
    )
    return jax.shard_map(
        on_device,
        mesh=mesh,
        in_specs=placed,
        out_specs=(P("row", None, "col"),) * 4,
        check_vma=False,
    )
```

time: 622 us -> 146 us (0.23); the launches traced: 612 us -> 146 us
  other arithmetic: 440 us -> 12.4 us
  Pallas kernels: 0 us -> 50.7 us
  matrix products: 36.5 us -> 0 us
  local copies, waits for them, and re-layouts: 22.2 us -> 2.75 us
  waiting for transfers between devices: 82.3 us -> 66.1 us
  between operations: 15.3 us -> 0.76 us
    another operation x41 -> x3, other arithmetic: 428 us -> 4.79 us  [the longest x1 4.73 us: on_device(): near = jnp.stack(around(near_blocks[:, 0], 'col'))]
    pallas_call x0 -> x3, Pallas kernels: none -> 50.7 us  [the longest x1 22.5 us: local_bases(): pl.pallas_call(functools.partial(local_kernel, columns), in_specs=[whole_...]
    dot_general x32 -> x0, matrix products: 21.8 us -> none  [the longest x28 11.6 us: product(): return jnp.matmul(left, right, precision=lax.Precision.HIGHEST)]
    all_gather x1 -> x0, waiting for transfers between devices: 16.5 us -> none  [on_device(): widened = lax.all_gather(edged_test, 'col', axis=0, tiled=True)]
    gather x4 -> x0, local copies, waits for them, and re-layouts: 15.5 us -> none  [the longest x2 7.76 us: on_device(): picked = jnp.take(widened, positions, axis=0)]
    ppermute x10 -> x9, waiting for transfers between devices: 51.1 us -> 66.1 us  [the longest x1 43.8 us: on_device(): low = lax.ppermute(test_panels, 'row', forward)]
    another operation x16 -> x0, matrix products: 14.7 us -> none  [the longest x7 5.23 us: combine(): jax.scipy.linalg.solve_triangular(factor, product(factor_a, panel_a) + pr...]
    psum x1 -> x0, waiting for transfers between devices: 14.6 us -> none  [on_device(): lax.psum(partial_value, 'col')]
  transfers between devices with their start and end apart: 12 -> 9, of which waited for: 7 -> 7; matrix products, arithmetic and copies ran while one was open for 46% -> 4% of each run, Pallas kernels for 0% -> 15%
where the time goes in v1:
time: 146 us
  waiting for transfers between devices  66.1 us (45%)
  Pallas kernels  50.7 us (35%)
  starting transfers between devices  13.1 us (9%)
  other arithmetic  12.4 us (8%)
  local copies, waits for them, and re-layouts  2.75 us (2%)
    ppermute x1, waiting for transfers between devices, on_device(): low = lax.ppermute(test_panels, 'row', forward)  43.8 us
    pallas_call x1, Pallas kernels, local_bases(): pl.pallas_call(functools.partial(local_kernel, columns), in_specs=[whole_...  22.5 us
    pallas_call x1, Pallas kernels, sampled(): pl.pallas_call(sample_kernel, grid_spec=grid, out_shape=[jax.ShapeDtypeSt...  15.7 us
    pallas_call x1, Pallas kernels, upper_bases(): pl.pallas_call(functools.partial(upper_kernel, columns, scale), in_specs=...  12.5 us
    ppermute x4, waiting for transfers between devices, on_device(): other = lax.ppermute(total, 'row', route)  12.5 us
    ppermute x3, waiting for transfers between devices, around(): parts.append(lax.ppermute(block, axis, route))  7.87 us
    ppermute x4, starting transfers between devices, on_device(): other = lax.ppermute(total, 'row', route)  6.23 us
    ppermute x1, starting transfers between devices, on_device(): low = lax.ppermute(test_panels, 'row', forward)  5.04 us
  transfers between devices with their start and end apart: 9, of which 7 were waited for; matrix products, arithmetic and copies ran while one was open for 4% of the time, Pallas kernels for 15%

profile of v1, /device:TPU:0, one launch (start us, length us, event | category | flops | bytes accessed | tf_op | source)
XLA Modules:
  0.0 145.8 jit_solution(9400067425875201685)
XLA Ops:
  0.6 0.0 copy-start.4
  0.6 0.0 copy-start.3
  0.7 5.0 %collective-permute-start.2 = (f32[4,256,256]{2,1,0:T(8,128)}, f32[4,256,256]{2,1,0:T(8,128)S(1)}, u32[]{:S(2)}, u32[]{:S(2)}) collective-permute-start(f32[4,256,256]{2,1,0:T(8,128)} %param.6), channel_id=1, source_target_pairs={{0,2},{2,4},{4,6},{6,8},{8,10},{10,12},{12,14},{14,16},{16,18},{18... | collective-permute-start | bytes 3145736 | tf_op jit(solution)/shard_map/ppermute | solution.py:243
  5.7 1.3 collective-permute-start.3
  7.0 43.8 %collective-permute-done.2 = f32[4,256,256]{2,1,0:T(8,128)S(1)} collective-permute-done((f32[4,256,256]{2,1,0:T(8,128)}, f32[4,256,256]{2,1,0:T(8,128)S(1)}, u32[]{:S(2)}, u32[]{:S(2)}) %collective-permute-start.2) | collective-permute-done | bytes 1048608 | tf_op jit(solution)/shard_map/ppermute | solution.py:243
  50.8 1.8 %collective-permute-done.3 = f32[4,256,256]{2,1,0:T(8,128)S(1)} collective-permute-done((f32[4,256,256]{2,1,0:T(8,128)}, f32[4,256,256]{2,1,0:T(8,128)S(1)}, u32[]{:S(2)}, u32[]{:S(2)}) %collective-permute-start.3) | collective-permute-done | bytes 1048608 | tf_op jit(solution)/shard_map/ppermute | solution.py:244
  52.7 3.1 %pad_maximum_fusion.2 = f32[12,256,256]{2,1,0:T(8,128)} fusion(f32[4,256,256]{2,1,0:T(8,128)S(1)} %collective-permute-done.3, f32[4,256,256]{2,1,0:T(8,128)} %param.6, f32[4,256,256]{2,1,0:T(8,128)S(1)} %collective-permute-done.2), kind=kLoop, calls=%fused_computation.2 | loop fusion | flops 1572864 | bytes 6291456 | tf_op jit(solution)/shard_map/concatenate | solution.py:245
  55.7 0.0 collective-permute-start.4
  55.7 0.5 collective-permute-start.1
  56.3 0.0 copy-done.4
  56.3 0.0 collective-permute-start
  56.3 0.0 copy-done.3
  56.3 0.4 copy.10.nugget
  56.7 4.7 %collective-permute-done = s32[8]{0:T(128)S(1)} collective-permute-done((s32[8]{0:T(128)S(1)}, s32[8]{0:T(128)S(1)}, u32[]{:S(2)}, u32[]{:S(2)}) %collective-permute-start) | collective-permute-done | bytes 64 | tf_op jit(solution)/shard_map/ppermute | solution.py:225
  61.4 0.1 copy.9
  61.5 0.1 reshape.197.place
  61.6 3.2 %collective-permute-done.1 = f32[8,256,256]{2,1,0:T(8,128)} collective-permute-done((f32[8,256,256]{2,1,0:T(8,128)}, f32[8,256,256]{2,1,0:T(8,128)}, u32[]{:S(2)}, u32[]{:S(2)}) %collective-permute-start.1) | collective-permute-done | bytes 2097184 | tf_op jit(solution)/shard_map/ppermute | solution.py:225
  64.7 0.0 copy-start.2
  64.8 4.7 %pad_maximum_fusion.1.near = f32[2,8,256,256]{3,2,1,0:T(8,128)} fusion(f32[1,8,256,256]{3,2,1,0:T(8,128)} %bitcast.6, f32[1,8,256,256]{3,2,1,0:T(8,128)} %bitcast.4), kind=kLoop, calls=%fused_computation.1 | loop fusion | flops 1048576 | bytes 8388608 | tf_op jit(solution)/shard_map/stack | solution.py:239
  69.5 0.0 collective-permute-done.4
  69.5 0.0 copy-done.2
  69.5 4.4 %pad_maximum_fusion.panels.own = f32[24,256,256]{2,1,0:T(8,128)} fusion(f32[12,256,256]{2,1,0:T(8,128)} %collective-permute-done.4, f32[4,256,256]{2,1,0:T(8,128)S(1)} %collective-permute-done.3, f32[4,256,256]{2,1,0:T(8,128)S(1)} %copy-done.2, f32[4,256,256]{2,1,0:T(8,128)S(1)} %collective-permute-done.2), kind=kLoop, calls=%fused_computation | loop fusion | flops 4718592 | bytes 12582912 | tf_op jit(solution)/shard_map/concatenate | solution.py:246
  73.9 15.7 %shard_map.75 = (f32[8,256,256]{2,1,0:T(8,128)S(1)}, f32[8,128,256]{2,1,0:T(8,128)S(1)}, f32[128,256]{1,0:T(8,128)S(1)}) custom-call(s32[24]{0:T(128)S(1)} %reshape.197.place, f32[2,8,256,256]{3,2,1,0:T(8,128)} %pad_maximum_fusion.1.near, f32[24,256,256]{2,1,0:T(8,128)} %pad_maximum_fusion.panels.own, f32[24,256,256]{2,1,0:T(8,128)} %pad_maximum_fusion.panels.own, ...), custom_call_target="tpu_custom_call" | custom-call | tf_op jit(solution)/shard_map/pallas_call | solution.py:123
  89.6 0.0 copy-start
  89.6 1.0 copy-done
  90.6 1.5 %collective-permute-start.5 = (f32[128,256]{1,0:T(8,128)S(1)}, f32[128,256]{1,0:T(8,128)S(1)}, u32[]{:S(2)}, u32[]{:S(2)}) collective-permute-start(f32[128,256]{1,0:T(8,128)S(1)} %get-tuple-element.15), channel_id=1, source_target_pairs={{0,2},{2,0},{4,6},{6,4},{8,10},{10,8},{12,14},{14,12},{16,18},{18,... | collective-permute-start | bytes 393224 | tf_op jit(solution)/shard_map/ppermute | solution.py:265
  92.1 4.2 %collective-permute-done.5 = f32[128,256]{1,0:T(8,128)S(1)} collective-permute-done((f32[128,256]{1,0:T(8,128)S(1)}, f32[128,256]{1,0:T(8,128)S(1)}, u32[]{:S(2)}, u32[]{:S(2)}) %collective-permute-start.5) | collective-permute-done | bytes 131104 | tf_op jit(solution)/shard_map/ppermute | solution.py:265
  96.3 0.1 collective-permute-start.6
  96.4 5.0 %collective-permute-done.6 = f32[128,256]{1,0:T(8,128)S(1)} collective-permute-done((f32[128,256]{1,0:T(8,128)S(1)}, f32[128,256]{1,0:T(8,128)S(1)}, u32[]{:S(2)}, u32[]{:S(2)}) %collective-permute-start.6) | collective-permute-done | bytes 131104 | tf_op jit(solution)/shard_map/ppermute | solution.py:265
  101.3 1.6 %collective-permute-start.7 = (f32[128,256]{1,0:T(8,128)S(1)}, f32[128,256]{1,0:T(8,128)S(1)}, u32[]{:S(2)}, u32[]{:S(2)}) collective-permute-start(f32[128,256]{1,0:T(8,128)S(1)} %add.166), channel_id=1, source_target_pairs={{0,8},{2,10},{4,12},{6,14},{8,0},{10,2},{12,4},{14,6},{16,24},{18,... | collective-permute-start | bytes 393224 | tf_op jit(solution)/shard_map/ppermute | solution.py:265
  103.0 3.4 %collective-permute-done.7 = f32[128,256]{1,0:T(8,128)S(1)} collective-permute-done((f32[128,256]{1,0:T(8,128)S(1)}, f32[128,256]{1,0:T(8,128)S(1)}, u32[]{:S(2)}, u32[]{:S(2)}) %collective-permute-start.7) | collective-permute-done | bytes 131104 | tf_op jit(solution)/shard_map/ppermute | solution.py:265
  106.4 3.0 %collective-permute-start.8 = (f32[128,256]{1,0:T(8,128)S(1)}, f32[128,256]{1,0:T(8,128)S(1)}, u32[]{:S(2)}, u32[]{:S(2)}) collective-permute-start(f32[128,256]{1,0:T(8,128)S(1)} %add.167), channel_id=1, source_target_pairs={{0,16},{2,18},{4,20},{6,22},{8,24},{10,26},{12,28},{14,30},{16,0},... | collective-permute-start | bytes 393224 | tf_op jit(solution)/shard_map/ppermute | solution.py:265
  109.4 0.0 copy-start.1
  109.4 1.2 copy-done.1
  110.6 22.5 %shard_map.76 = (f32[8,128,128]{2,1,0:T(8,128)}, f32[8,128,128]{2,1,0:T(8,128)}, f32[7,128,128]{2,1,0:T(8,128)}) custom-call(f32[8,256,256]{2,1,0:T(8,128)S(1)} %get-tuple-element.10.sample, f32[8,128,256]{2,1,0:T(8,128)S(1)} %copy-done.1), custom_call_target="tpu_custom_call" | custom-call | flops 10000000000 | bytes 4000000 | tf_op jit(solution)/shard_map/pallas_call | solution.py:187
  133.1 0.0 collective-permute-done.8
  133.2 12.5 %shard_map.77 = f32[1,128,128]{2,1,0:T(8,128)} custom-call(f32[2,128,128]{2,1,0:T(8,128)S(1)} %pad_maximum_fusion.3.pair, f32[128,128]{1,0:T(8,128)S(1)} %constant_dynamic-slice_fusion.root), custom_call_target="tpu_custom_call" | custom-call | tf_op jit(solution)/shard_map/pallas_call | solution.py:210
  (10 shorter events, 0.2 us)
Async XLA Ops:
  0.6 55.6 %copy-start.4 = (s32[8,1]{0,1:T(1,128)S(1)}, s32[8,1]{0,1:T(1,128)}, u32[]{:S(2)}) copy-start(s32[8,1]{0,1:T(1,128)} %param.5) | copy-start | bytes 100
  0.6 55.6 %copy-start.3 = (f32[8,256]{1,0:T(8,128)S(1)}, f32[8,256]{1,0:T(8,128)}, u32[]{:S(2)}) copy-start(f32[8,256]{1,0:T(8,128)} %param.7) | copy-start | bytes 24580
  0.7 50.2 %collective-permute-start.2 = (f32[4,256,256]{2,1,0:T(8,128)}, f32[4,256,256]{2,1,0:T(8,128)S(1)}, u32[]{:S(2)}, u32[]{:S(2)}) collective-permute-start(f32[4,256,256]{2,1,0:T(8,128)} %param.6), channel_id=1, source_target_pairs={{0,2},{2,4},{4,6},{6,8},{8,10},{10,12},{12,14},{14,16},{16,18},{18... | collective-permute-start | bytes 3145736 | tf_op jit(solution)/shard_map/ppermute | solution.py:243
  5.7 47.0 %collective-permute-start.3 = (f32[4,256,256]{2,1,0:T(8,128)}, f32[4,256,256]{2,1,0:T(8,128)S(1)}, u32[]{:S(2)}, u32[]{:S(2)}) collective-permute-start(f32[4,256,256]{2,1,0:T(8,128)} %param.6), channel_id=1, source_target_pairs={{2,0},{4,2},{6,4},{8,6},{10,8},{12,10},{14,12},{16,14},{18,16},{20... | collective-permute-start | bytes 3145736 | tf_op jit(solution)/shard_map/ppermute | solution.py:244
  55.7 13.7 %collective-permute-start.4 = (f32[12,256,256]{2,1,0:T(8,128)}, f32[12,256,256]{2,1,0:T(8,128)}, u32[]{:S(2)}, u32[]{:S(2)}) collective-permute-start(f32[12,256,256]{2,1,0:T(8,128)} %pad_maximum_fusion.2), channel_id=1, source_target_pairs={{1,0},{0,1},{3,2},{2,3},{5,4},{4,5},{7,6},{6,7},{9,8},{8,9},{11,10... | collective-permute-start | bytes 9437192 | tf_op jit(solution)/shard_map/ppermute | solution.py:225
  55.7 9.0 %collective-permute-start.1 = (f32[8,256,256]{2,1,0:T(8,128)}, f32[8,256,256]{2,1,0:T(8,128)}, u32[]{:S(2)}, u32[]{:S(2)}) collective-permute-start(f32[8,256,256]{2,1,0:T(8,128)} %bitcast.5), channel_id=1, source_target_pairs={{1,0},{0,1},{3,2},{2,3},{5,4},{4,5},{7,6},{6,7},{9,8},{8,9},{11,10... | collective-permute-start | bytes 6291464 | tf_op jit(solution)/shard_map/ppermute | solution.py:225
  56.3 5.1 %collective-permute-start = (s32[8]{0:T(128)S(1)}, s32[8]{0:T(128)S(1)}, u32[]{:S(2)}, u32[]{:S(2)}) collective-permute-start(s32[8]{0:T(128)S(1)} %bitcast.14), channel_id=1, source_target_pairs={{1,0},{0,1},{3,2},{2,3},{5,4},{4,5},{7,6},{6,7},{9,8},{8,9},{11,10... | collective-permute-start | bytes 104 | tf_op jit(solution)/shard_map/ppermute | solution.py:225
  64.7 4.7 %copy-start.2 = (f32[4,256,256]{2,1,0:T(8,128)S(1)}, f32[4,256,256]{2,1,0:T(8,128)}, u32[]{:S(2)}) copy-start(f32[4,256,256]{2,1,0:T(8,128)} %param.6) | copy-start | bytes 3145732
  89.6 1.0 copy-start
  90.6 5.7 %collective-permute-start.5 = (f32[128,256]{1,0:T(8,128)S(1)}, f32[128,256]{1,0:T(8,128)S(1)}, u32[]{:S(2)}, u32[]{:S(2)}) collective-permute-start(f32[128,256]{1,0:T(8,128)S(1)} %get-tuple-element.15), channel_id=1, source_target_pairs={{0,2},{2,0},{4,6},{6,4},{8,10},{10,8},{12,14},{14,12},{16,18},{18,... | collective-permute-start | bytes 393224 | tf_op jit(solution)/shard_map/ppermute | solution.py:265
  96.3 5.0 %collective-permute-start.6 = (f32[128,256]{1,0:T(8,128)S(1)}, f32[128,256]{1,0:T(8,128)S(1)}, u32[]{:S(2)}, u32[]{:S(2)}) collective-permute-start(f32[128,256]{1,0:T(8,128)S(1)} %add.165), channel_id=1, source_target_pairs={{0,4},{2,6},{4,0},{6,2},{8,12},{10,14},{12,8},{14,10},{16,20},{18,... | collective-permute-start | bytes 393224 | tf_op jit(solution)/shard_map/ppermute | solution.py:265
  101.3 5.0 %collective-permute-start.7 = (f32[128,256]{1,0:T(8,128)S(1)}, f32[128,256]{1,0:T(8,128)S(1)}, u32[]{:S(2)}, u32[]{:S(2)}) collective-permute-start(f32[128,256]{1,0:T(8,128)S(1)} %add.166), channel_id=1, source_target_pairs={{0,8},{2,10},{4,12},{6,14},{8,0},{10,2},{12,4},{14,6},{16,24},{18,... | collective-permute-start | bytes 393224 | tf_op jit(solution)/shard_map/ppermute | solution.py:265
  106.4 26.7 %collective-permute-start.8 = (f32[128,256]{1,0:T(8,128)S(1)}, f32[128,256]{1,0:T(8,128)S(1)}, u32[]{:S(2)}, u32[]{:S(2)}) collective-permute-start(f32[128,256]{1,0:T(8,128)S(1)} %add.167), channel_id=1, source_target_pairs={{0,16},{2,18},{4,20},{6,22},{8,24},{10,26},{12,28},{14,30},{16,0},... | collective-permute-start | bytes 393224 | tf_op jit(solution)/shard_map/ppermute | solution.py:265
  109.4 1.2 copy-start.1

commit v2 on v1

v2 whole, which is shorter than its diff:
```python
import functools
import math

import jax
import jax.numpy as jnp
from jax import lax
from jax.experimental import pallas as pl
from jax.experimental.pallas import tpu as pltpu
from jax.sharding import PartitionSpec as P

STRIP = 32
SLAB = 8
CUTS = 2
LIMIT = 48 * 1024 * 1024


def dot(left, right, left_dim, right_dim):
    return lax.dot_general(
        left,
        right,
        (((left_dim,), (right_dim,)), ((), ())),
        precision=lax.Precision.HIGHEST,
        preferred_element_type=jnp.float32,
    )


def load_augmented(work, slot, gram):
    size = gram.shape[0]
    row = lax.broadcasted_iota(jnp.int32, (size, size), 0)
    lane = lax.broadcasted_iota(jnp.int32, (size, size), 1)
    work[slot, :, :size] = gram
    work[slot, :, size:] = jnp.where(row == lane, 1.0, 0.0)


def eliminate(work, first, count):
    size = work.shape[1]
    row = lax.broadcasted_iota(jnp.int32, (count, SLAB, 1), 1)
    lane = lax.broadcasted_iota(jnp.int32, (1, SLAB, 2 * size), 2)
    sub = lax.broadcasted_iota(jnp.int32, (1, SLAB, 2 * size), 1)
    own = pl.ds(first, count)
    for top in range(0, size, STRIP):
        slabs = [
            work[own, top + at : top + at + SLAB, :] for at in range(0, STRIP, SLAB)
        ]
        for step in range(STRIP):
            at, inner = divmod(step, SLAB)
            here = top + step
            column = slabs[at][:, :, here : here + 1]
            pivot_row = slabs[at][:, inner : inner + 1, :]
            pivot = column[:, inner : inner + 1, :]
            scaled = pivot_row * (1.0 / pivot)
            for later in range(at, len(slabs)):
                if later == at:
                    if inner == SLAB - 1:
                        continue
                    factor = jnp.where(row > inner, column, 0.0)
                else:
                    factor = slabs[later][:, :, here : here + 1]
                slabs[later] = slabs[later] - factor * scaled
        done = []
        for at, slab in enumerate(slabs):
            base = top + at * SLAB
            diagonal = jnp.sum(
                jnp.where(lane == sub + base, slab, 0.0), axis=2, keepdims=True
            )
            slab = slab * lax.rsqrt(diagonal)
            slab = jnp.where(lane >= sub + base, slab, 0.0)
            work[own, base : base + SLAB, :] = slab
        below = top + STRIP
        if below < size:
            for slot in range(first, first + count):
                strip = work[slot, top:below, :]
                work[slot, below:, :] -= dot(strip[:, below:size], strip, 0, 0)


def peer(**place):
    return dict(device_id=place, device_id_type=pl.DeviceIdType.MESH)


def gather_kernel(
    rows, columns, pick, flag, near, test, nugget,
    sample, moments, pair, root,
    panels, blocks, sums, inbox,
    send_x, recv_x, send_y, recv_y, send_z, recv_z,
    send_c, recv_c, send_own, recv_own, send_near, recv_near, send_up, recv_up, here_sem,
):
    row, column = lax.axis_index("row"), lax.axis_index("col")
    leaves, size = near.shape[1], near.shape[2]
    piece = test.shape[0]
    width = moments.shape[1]
    levels = rows.bit_length() - 1
    corner = row % 4
    ends = jnp.logical_or(corner == 0, corner == 3)
    above = jnp.logical_and(ends, row + 4 < rows)
    below = jnp.logical_and(ends, row >= 4)
    z_out = jnp.where(corner == 0, row + 4, row - 4)
    has_out = jnp.where(corner == 0, above, below)
    has_in = jnp.where(corner == 0, below, above)

    barrier = pltpu.get_barrier_semaphore()
    for level in range(levels):
        pl.semaphore_signal(barrier, inc=1, **peer(row=row ^ (1 << level)))
    for shift in range(1, columns):
        pl.semaphore_signal(barrier, inc=1, **peer(col=(column + shift) % columns))

    @pl.when(above)
    def _():
        pl.semaphore_signal(barrier, inc=1, **peer(row=row + 4))

    @pl.when(below)
    def _():
        pl.semaphore_signal(barrier, inc=1, **peer(row=row - 4))

    extra = above.astype(jnp.int32) + below.astype(jnp.int32)
    pl.semaphore_wait(barrier, levels + columns - 1 + extra)

    cuts = CUTS
    part_rows = size // cuts
    chunks = piece * cuts

    def part(ref, *lead_and_chunk):
        *lead, chunk = lead_and_chunk
        at, cut = divmod(chunk, cuts)
        return ref.at[(*lead, at, pl.ds(cut * part_rows, part_rows))]

    def along(source, kind, chunk, send, recv, target):
        return pltpu.make_async_remote_copy(
            src_ref=source, dst_ref=part(panels, 0, kind, chunk),
            send_sem=send.at[chunk], recv_sem=recv.at[chunk], **peer(row=target),
        )

    def x_copy(chunk):
        return along(part(test, chunk), 1, chunk, send_x, recv_x, row ^ 1)

    def y_copy(chunk):
        return along(part(panels, 0, 1, chunk), 2, chunk, send_y, recv_y, row ^ 2)

    def z_copy(chunk):
        return along(part(panels, 0, 2, chunk), 3, chunk, send_z, recv_z, z_out)

    def c_copy(shift, kind, lane, chunk):
        return pltpu.make_async_remote_copy(
            src_ref=part(panels, 0, kind, chunk),
            dst_ref=part(panels, shift, kind, chunk),
            send_sem=send_c.at[shift - 1, lane, chunk],
            recv_sem=recv_c.at[shift - 1, lane, chunk],
            **peer(col=(column + shift) % columns),
        )

    def own_copy(shift):
        return pltpu.make_async_remote_copy(
            src_ref=test, dst_ref=panels.at[shift, 0],
            send_sem=send_own.at[shift - 1], recv_sem=recv_own.at[shift - 1],
            **peer(col=(column + shift) % columns),
        )

    def near_copy(shift):
        return pltpu.make_async_remote_copy(
            src_ref=near.at[0], dst_ref=blocks.at[shift],
            send_sem=send_near.at[shift - 1], recv_sem=recv_near.at[shift - 1],
            **peer(col=(column + shift) % columns),
        )

    shifts = range(1, columns)
    for chunk in range(chunks):
        x_copy(chunk).start()
    for shift in shifts:
        own_copy(shift).start()
        near_copy(shift).start()
    own_test = pltpu.make_async_copy(test, panels.at[0, 0], here_sem.at[0])
    own_near = pltpu.make_async_copy(near.at[0], blocks.at[0], here_sem.at[1])
    own_test.start()
    own_near.start()
    for step in range(chunks + 2):
        if step < chunks:
            x_copy(step).wait_recv()
            y_copy(step).start()
            for shift in shifts:
                c_copy(shift, 1, 0, step).start()
        if 1 <= step <= chunks:
            chunk = step - 1
            y_copy(chunk).wait_recv()

            @pl.when(has_out)
            def _():
                z_copy(chunk).start()

            @pl.when(jnp.logical_not(ends))
            def _():
                for shift in shifts:
                    c_copy(shift, 2, 1, chunk).start()

        if step >= 2:
            chunk = step - 2

            @pl.when(has_in)
            def _():
                z_copy(chunk).wait_recv()
                for shift in shifts:
                    c_copy(shift, 3, 1, chunk).start()

    for chunk in range(chunks):
        x_copy(chunk).wait_send()
        y_copy(chunk).wait_send()
        for shift in shifts:
            c_copy(shift, 1, 0, chunk).wait()

        @pl.when(has_out)
        def _():
            z_copy(chunk).wait_send()

        @pl.when(jnp.logical_not(ends))
        def _():
            for shift in shifts:
                c_copy(shift, 2, 1, chunk).wait()

        @pl.when(has_in)
        def _():
            for shift in shifts:
                c_copy(shift, 3, 1, chunk).wait()

    for shift in shifts:
        own_copy(shift).wait()
        near_copy(shift).wait()
    own_test.wait()
    own_near.wait()

    diagonal = lax.broadcasted_iota(jnp.int32, (size, size), 0) == lax.broadcasted_iota(
        jnp.int32, (size, size), 1
    )
    sums[0] = jnp.zeros_like(sums[0])

    @pl.loop(0, leaves)
    def _(leaf):
        variance = jnp.where(diagonal, nugget[leaf], 0.0)
        whole = jnp.zeros((size, 2 * width), jnp.float32)
        for slot in range(columns):
            at = slot * leaves + leaf
            whole += dot(blocks[slot, leaf] + variance * flag[at], panels[
                pick[3 * at], pick[3 * at + 1], pick[3 * at + 2]], 1, 0)
        sample[leaf] = whole
        both = dot(whole[:, :width], whole, 0, 0)
        moments[leaf] = both
        sums[0] += both

    for level in range(levels):
        stride = 1 << level
        up = pltpu.make_async_remote_copy(
            src_ref=sums.at[level], dst_ref=inbox.at[level],
            send_sem=send_up.at[level], recv_sem=recv_up.at[level], **peer(row=row ^ stride),
        )
        up.start()
        up.wait()
        both = sums[level] + inbox[level]
        sums[level + 1] = both

        @pl.when(row % (2 * stride) == stride)
        def _():
            left = (column * 2) // columns == 0
            pair[0] = both[:, :width]
            pair[1] = jnp.where(left, inbox[level], sums[level])[:, :width]

    root[...] = sums[levels]

    @pl.when(row == 0)
    def _():
        pair[0] = sums[levels, :, :width]
        pair[1] = sums[levels, :, :width]


def gathered(pick, flag, near, test, nugget, rows, columns):
    leaves, size = near.shape[1], near.shape[2]
    piece, wide = test.shape[0], test.shape[2]
    width = wide // 2
    levels = rows.bit_length() - 1
    chunks = piece * CUTS
    f32 = jnp.float32
    dma = pltpu.SemaphoreType.DMA
    smem = pl.BlockSpec(memory_space=pltpu.SMEM)
    anywhere = pl.BlockSpec(memory_space=pl.ANY)
    return pl.pallas_call(
        functools.partial(gather_kernel, rows, columns),
        in_specs=[smem, smem, anywhere, anywhere, whole_spec()],
        out_specs=[whole_spec()] * 4,
        out_shape=[
            jax.ShapeDtypeStruct((leaves, size, wide), f32),
            jax.ShapeDtypeStruct((leaves, width, wide), f32),
            jax.ShapeDtypeStruct((2, width, width), f32),
            jax.ShapeDtypeStruct((width, wide), f32),
        ],
        scratch_shapes=[
            pltpu.VMEM((columns, 4, piece, size, wide), f32),
            pltpu.VMEM((columns, leaves, size, size), f32),
            pltpu.VMEM((levels + 1, width, wide), f32),
            pltpu.VMEM((levels, width, wide), f32),
        ]
        + [dma((chunks,))] * 6
        + [dma((columns - 1, 2, chunks))] * 2
        + [dma((columns - 1,))] * 4
        + [dma((levels,))] * 2
        + [dma((2,))],
        compiler_params=pltpu.CompilerParams(
            vmem_limit_bytes=LIMIT, collective_id=0, has_side_effects=True
        ),
    )(pick, flag, near, test, nugget)


def bases_kernel(
    columns, scale, sample, moments, pair, root, basis, missed, inner, upper, work, sums
):
    leaves, width, wide = moments.shape
    share = wide // columns
    column = lax.axis_index("col")
    side = column * share // width
    offset = pl.multiple_of(column * share % width, share)
    nodes = 2 * leaves - 1
    for leaf in range(leaves):
        sums[leaf] = moments[leaf, :, :width]
    for node in range(leaves, nodes):
        child = 2 * (node - leaves)
        sums[node] = sums[child] + sums[child + 1]
    for node in range(nodes):
        load_augmented(work, node, sums[node])
    load_augmented(work, nodes, pair[0])
    load_augmented(work, nodes + 1, pair[1])
    eliminate(work, 0, nodes + 2)
    points = pl.ds(pl.multiple_of(column * share, share), share)
    for leaf in range(leaves):
        inverse = work[leaf, :, width:]
        part = sample[leaf, points, :]
        own = dot(inverse, part[:, :width], 1, 1)
        basis[leaf] = own
        reduced = dot(inverse, moments[leaf, :, width:], 1, 0)
        missed[leaf] = part[:, width:].T - dot(reduced, own, 0, 0)
    for node in range(leaves, nodes):
        child = 2 * (node - leaves) + side
        inner[node - leaves] = dot(
            work[node, :, width:], work[child, pl.ds(offset, share), :width], 1, 1
        )
    inverse = work[nodes, :, width:]
    node = dot(inverse, work[nodes + 1, pl.ds(offset, share), :width], 1, 1)
    top = dot(inverse, root[...], 1, 0) * scale
    upper[0] = jnp.where(lax.axis_index("row") == 0, top, node)


def whole_spec():
    return pl.BlockSpec(memory_space=pltpu.VMEM)


def bases(sample, moments, pair, root, columns, scale):
    leaves, width, wide = moments.shape
    share = wide // columns
    nodes = 2 * leaves - 1
    counts = (leaves, leaves, leaves - 1, 1)
    return pl.pallas_call(
        functools.partial(bases_kernel, columns, scale),
        in_specs=[whole_spec()] * 4,
        out_specs=[whole_spec()] * 4,
        out_shape=[
            jax.ShapeDtypeStruct((count, width, share), jnp.float32) for count in counts
        ],
        scratch_shapes=[
            pltpu.VMEM((nodes + 2, width, wide), jnp.float32),
            pltpu.VMEM((nodes, width, width), jnp.float32),
        ],
        compiler_params=pltpu.CompilerParams(vmem_limit_bytes=LIMIT),
    )(sample, moments, pair, root)


def around(block, axis):
    count = lax.axis_size(axis)
    parts = [block]
    for shift in range(1, count):
        route = [((i + shift) % count, i) for i in range(count)]
        parts.append(lax.ppermute(block, axis, route))
    return parts


def on_device(near_blocks, column_block, test_panels, nugget):
    leaves = near_blocks.shape[0]
    block = near_blocks.shape[2]
    width = test_panels.shape[2] // 2
    piece = test_panels.shape[0]
    row = lax.axis_index("row")
    column = lax.axis_index("col")
    rows = lax.axis_size("row")
    columns = lax.axis_size("col")

    choice = jnp.stack(around(column_block[:, 0], "col"))
    first = row * leaves
    place = choice - first + leaves
    part, within = place // leaves, place % leaves
    corner = row % 4
    low = jnp.where(corner == 0, 3, jnp.where(corner == 2, 2, 1))
    high = jnp.where(corner == 3, 3, jnp.where(corner == 1, 2, 1))
    kind = jnp.where(part == 0, low, jnp.where(part == 1, 0, high))
    shift = (column - within // piece + columns) % columns
    pick = jnp.stack([shift, kind, within % piece], axis=-1).reshape(-1)
    own = first + jnp.arange(leaves, dtype=jnp.int32)
    flag = (choice == own).astype(jnp.float32).reshape(-1)
    sample, moments, pair, root = gathered(
        pick, flag, near_blocks.swapaxes(0, 1), test_panels, nugget[:, None], rows, columns
    )
    share = 2 * width // columns
    root = lax.dynamic_slice_in_dim(root, column * share, share, 1)
    scale = 1.0 / math.sqrt(leaves * rows * block)
    return tuple(bases(sample, moments, pair, root, columns, scale))


def solution(mesh):
    placed = (
        P("row", "col", None, None),
        P("row", "col"),
        P(("row", "col"), None, None),
        P("row", None),
    )
    return jax.shard_map(
        on_device,
        mesh=mesh,
        in_specs=placed,
        out_specs=(P("row", None, "col"),) * 4,
        check_vma=False,
    )
```

time: 146 us -> 96.4 us (0.66)
  waiting for transfers between devices: 66.1 us -> 0.25 us
  Pallas kernels: 50.7 us -> 90.5 us
  starting transfers between devices: 13.1 us -> 0.52 us
  other arithmetic: 12.4 us -> 2.04 us
    ppermute x6 -> x0, waiting for transfers between devices: 58.2 us -> none  [the longest x1 43.8 us: on_device(): low = lax.ppermute(test_panels, 'row', forward)]
    pallas_call x3 -> x2, Pallas kernels: 50.7 us -> 90.5 us  [the longest x1 68 us: gathered(): pl.pallas_call(functools.partial(gather_kernel, rows, columns), in_specs=...]
    ppermute x6 -> x0, starting transfers between devices: 12.6 us -> none  [the longest x4 6.23 us: on_device(): other = lax.ppermute(total, 'row', route)]
    ppermute x3 -> x1, waiting for transfers between devices: 7.87 us -> 0.25 us  [around(): parts.append(lax.ppermute(block, axis, route))]
    concatenate x3 -> x0, other arithmetic: 7.51 us -> none  [the longest x1 4.41 us: on_device(): panels = jnp.concatenate(around(panels, 'col'), axis=0)]
    another operation x3 -> x1, other arithmetic: 4.79 us -> 0.01 us  [on_device(): pick = jnp.stack([shift, kind, within % piece], axis=-1).reshape(-1)]
  transfers between devices with their start and end apart: 9 -> 1, of which waited for: 7 -> 1; matrix products, arithmetic and copies ran while one was open for 4% -> 1% of each run, Pallas kernels for 15% -> 0%
where the time goes in v2:
time: 96.4 us; the launch traced here: 96.2 us
  Pallas kernels  90.5 us (94%)
  local copies, waits for them, and re-layouts  2.2 us (2%)
  other arithmetic  2.04 us (2%)
    pallas_call x1, Pallas kernels, gathered(): pl.pallas_call(functools.partial(gather_kernel, rows, columns), in_specs=...  68 us
    pallas_call x1, Pallas kernels, bases(): pl.pallas_call(functools.partial(bases_kernel, columns, scale), in_specs=...  22.5 us
  transfers between devices with their start and end apart: 1, of which 1 were waited for; matrix products, arithmetic and copies ran while one was open for 1% of the time, Pallas kernels for 0%

profile of v2, /device:TPU:0, one launch (start us, length us, event | category | flops | bytes accessed | tf_op | source)
XLA Modules:
  0.0 96.2 jit_solution(2455488760451772531)
XLA Ops:
  0.6 0.5 collective-permute-start
  1.2 0.7 broadcast_in_dim.16.nugget
  1.9 0.2 collective-permute-done
  2.1 0.7 compare_convert_fusion
  2.8 0.1 reshape.267.flag
  2.9 0.7 and_select_fusion.2
  3.5 0.7 and_select_fusion
  4.2 0.1 copy.9
  4.3 0.1 reshape.266.pick
  4.4 0.0 copy-start
  4.4 1.2 %copy-done = f32[4,256,256]{2,1,0:T(8,128)S(1)} copy-done((f32[4,256,256]{2,1,0:T(8,128)S(1)}, f32[4,256,256]{2,1,0:T(8,128)}, u32[]{:S(2)}) %copy-start) | copy-done | bytes 1048600
  5.6 68.0 %shard_map.75 = (f32[8,256,256]{2,1,0:T(8,128)S(1)}, f32[8,128,256]{2,1,0:T(8,128)S(1)}, f32[2,128,128]{2,1,0:T(8,128)S(1)}, f32[128,256]{1,0:T(8,128)S(1)}) custom-call(s32[48]{0:T(128)S(1)} %reshape.266.pick, f32[16]{0:T(128)S(1)} %reshape.267.flag, f32[1,8,256,256]{3,2,1,0:T(8,128)} %bitcast.6, f32[4,256,256]{2,1,0:T(8,128)S(1)} %copy-done, ...), custom_call_target="tpu_custom_call" | custom-call | tf_op jit(solution)/shard_map/pallas_call | solution.py:281
  73.7 22.5 %shard_map.76 = (f32[8,128,128]{2,1,0:T(8,128)}, f32[8,128,128]{2,1,0:T(8,128)}, f32[7,128,128]{2,1,0:T(8,128)}, f32[1,128,128]{2,1,0:T(8,128)}) custom-call(f32[8,256,256]{2,1,0:T(8,128)S(1)} %get-tuple-element.8.sample, f32[8,128,256]{2,1,0:T(8,128)S(1)} %get-tuple-element.9.moments, f32[2,128,128]{2,1,0:T(8,128)S(1)} %get-tuple-element.10.pair, ...), custom_call_target="tpu_custom_call" | custom-call | tf_op jit(solution)/shard_map/pallas_call | solution.py:355
  (3 shorter events, 0.0 us)
Async XLA Ops:
  0.6 1.5 %collective-permute-start = (s32[8]{0:T(128)}, s32[8]{0:T(128)S(1)}, u32[]{:S(2)}, u32[]{:S(2)}) collective-permute-start(s32[8]{0:T(128)} %bitcast.7), channel_id=1, source_target_pairs={{1,0},{0,1},{3,2},{2,3},{5,4},{4,5},{7,6},{6,7},{9,8},{8,9},{11,10... | collective-permute-start | bytes 104 | tf_op jit(solution)/shard_map/ppermute | solution.py:375
  4.4 1.2 %copy-start = (f32[4,256,256]{2,1,0:T(8,128)S(1)}, f32[4,256,256]{2,1,0:T(8,128)}, u32[]{:S(2)}) copy-start(f32[4,256,256]{2,1,0:T(8,128)} %test.1) | copy-start | bytes 3145732

commit v3 on v2

v3 whole, which is shorter than its diff:
```python
import functools
import math

import jax
import jax.numpy as jnp
from jax import lax
from jax.experimental import pallas as pl
from jax.experimental.pallas import tpu as pltpu
from jax.sharding import PartitionSpec as P

STRIP = 32
SLAB = 8
CUTS = 2
GROUP = 2
LIMIT = 48 * 1024 * 1024


def dot(left, right, left_dim, right_dim):
    return lax.dot_general(
        left,
        right,
        (((left_dim,), (right_dim,)), ((), ())),
        precision=lax.Precision.HIGHEST,
        preferred_element_type=jnp.float32,
    )


def load_augmented(work, slot, gram):
    size = gram.shape[0]
    row = lax.broadcasted_iota(jnp.int32, (size, size), 0)
    lane = lax.broadcasted_iota(jnp.int32, (size, size), 1)
    work[slot, :, :size] = gram
    work[slot, :, size:] = jnp.where(row == lane, 1.0, 0.0)


def split(value):
    high = value.astype(jnp.bfloat16)
    return high, (value - high.astype(jnp.float32)).astype(jnp.bfloat16)


def dot_three(left, right, left_dim, right_dim):
    def one(a, b):
        return lax.dot_general(
            a, b, (((left_dim,), (right_dim,)), ((), ())), preferred_element_type=jnp.float32
        )

    left_high, left_low = split(left)
    right_high, right_low = split(right)
    return one(left_high, right_high) + (one(left_high, right_low) + one(left_low, right_high))


def eliminate_strip(work, first, count, top):
    size = work.shape[1]
    row = lax.broadcasted_iota(jnp.int32, (1, SLAB, size), 1)
    lane = lax.broadcasted_iota(jnp.int32, (1, SLAB, size), 2)
    own = pl.ds(first, count)
    shape = (count, SLAB, size)

    def spread(value):
        return jnp.broadcast_to(value, shape)

    slabs = [
        [
            work[own, top + at : top + at + SLAB, half : half + size]
            for half in (0, size)
        ]
        for at in range(0, STRIP, SLAB)
    ]
    for step in range(0, STRIP, GROUP):
        at, inner = divmod(step, SLAB)
        here = top + step
        columns = {
            later: [
                spread(slabs[later][0][:, :, here + k : here + k + 1]) for k in range(GROUP)
            ]
            for later in range(at, len(slabs))
        }
        pivots = [
            [
                spread(columns[at][k][:, inner + m : inner + m + 1, :]) if m >= k else None
                for m in range(GROUP)
            ]
            for k in range(GROUP)
        ]
        rows = [
            [spread(half[:, inner + k : inner + k + 1, :]) for half in slabs[at]]
            for k in range(GROUP)
        ]
        for k in range(GROUP):
            inverse = 1.0 / pivots[k][k]
            lower = {m: pivots[k][m] * inverse for m in range(k + 1, GROUP)}
            for t in range(k + 1, GROUP):
                for m in range(t, GROUP):
                    pivots[t][m] = pivots[t][m] - pivots[k][m] * lower[t]
                rows[t] = [x - lower[t] * y for x, y in zip(rows[t], rows[k])]
                for later in columns:
                    columns[later][t] = columns[later][t] - columns[later][k] * lower[t]
            scaled = [half * inverse for half in rows[k]]
            for later in columns:
                factor = columns[later][k]
                if later == at:
                    if inner + k == SLAB - 1:
                        continue
                    factor = jnp.where(row > inner + k, factor, 0.0)
                slabs[later] = [x - factor * y for x, y in zip(slabs[later], scaled)]
    for at, slab in enumerate(slabs):
        base = top + at * SLAB
        diagonal = jnp.sum(
            jnp.where(lane == row + base, slab[0], 0.0), axis=2, keepdims=True
        )
        scale = lax.rsqrt(diagonal)
        work[own, base : base + SLAB, :size] = jnp.where(lane >= row + base, slab[0] * scale, 0.0)
        work[own, base : base + SLAB, size:] = slab[1] * scale
    below = top + STRIP
    if below < size:
        for slot in range(first, first + count):
            strip = work[slot, top:below, :]
            work[slot, below:, :] -= dot(strip[:, below:size], strip, 0, 0)


def peer(**place):
    return dict(device_id=place, device_id_type=pl.DeviceIdType.MESH)


def sweep_kernel(
    rows, columns, scale, choice, near, test, nugget,
    basis, missed, inner_basis, upper,
    panels, blocks, sample, moments, sums, inbox, grams, work, pair,
    send_x, recv_x, send_y, recv_y, send_z, recv_z,
    send_c, recv_c, send_own, recv_own, send_near, recv_near, send_up, recv_up, here_sem,
):
    row, column = lax.axis_index("row"), lax.axis_index("col")
    leaves, size = near.shape[1], near.shape[2]
    piece = test.shape[0]
    width = moments.shape[1]
    levels = rows.bit_length() - 1
    corner = row % 4
    ends = jnp.logical_or(corner == 0, corner == 3)
    above = jnp.logical_and(ends, row + 4 < rows)
    below = jnp.logical_and(ends, row >= 4)
    z_out = jnp.where(corner == 0, row + 4, row - 4)
    has_out = jnp.where(corner == 0, above, below)
    has_in = jnp.where(corner == 0, below, above)

    barrier = pltpu.get_barrier_semaphore()
    for level in range(levels):
        pl.semaphore_signal(barrier, inc=1, **peer(row=row ^ (1 << level)))
    for shift in range(1, columns):
        pl.semaphore_signal(barrier, inc=1, **peer(col=(column + shift) % columns))

    @pl.when(above)
    def _():
        pl.semaphore_signal(barrier, inc=1, **peer(row=row + 4))

    @pl.when(below)
    def _():
        pl.semaphore_signal(barrier, inc=1, **peer(row=row - 4))

    extra = above.astype(jnp.int32) + below.astype(jnp.int32)
    pl.semaphore_wait(barrier, levels + columns - 1 + extra)

    cuts = CUTS
    part_rows = size // cuts
    chunks = piece * cuts

    def part(ref, *lead_and_chunk):
        *lead, chunk = lead_and_chunk
        at, cut = divmod(chunk, cuts)
        return ref.at[(*lead, at, pl.ds(cut * part_rows, part_rows))]

    def along(source, kind, chunk, send, recv, target):
        return pltpu.make_async_remote_copy(
            src_ref=source, dst_ref=part(panels, 0, kind, chunk),
            send_sem=send.at[chunk], recv_sem=recv.at[chunk], **peer(row=target),
        )

    def x_copy(chunk):
        return along(part(test, chunk), 1, chunk, send_x, recv_x, row ^ 1)

    def y_copy(chunk):
        return along(part(panels, 0, 1, chunk), 2, chunk, send_y, recv_y, row ^ 2)

    def z_copy(chunk):
        return along(part(panels, 0, 2, chunk), 3, chunk, send_z, recv_z, z_out)

    def c_copy(shift, kind, lane, chunk):
        return pltpu.make_async_remote_copy(
            src_ref=part(panels, 0, kind, chunk),
            dst_ref=part(panels, shift, kind, chunk),
            send_sem=send_c.at[shift - 1, lane, chunk],
            recv_sem=recv_c.at[shift - 1, lane, chunk],
            **peer(col=(column + shift) % columns),
        )

    def own_copy(shift):
        return pltpu.make_async_remote_copy(
            src_ref=test, dst_ref=panels.at[shift, 0],
            send_sem=send_own.at[shift - 1], recv_sem=recv_own.at[shift - 1],
            **peer(col=(column + shift) % columns),
        )

    def near_copy(shift):
        return pltpu.make_async_remote_copy(
            src_ref=near.at[0], dst_ref=blocks.at[shift],
            send_sem=send_near.at[shift - 1], recv_sem=recv_near.at[shift - 1],
            **peer(col=(column + shift) % columns),
        )

    shifts = range(1, columns)
    for chunk in range(chunks):
        x_copy(chunk).start()
    for shift in shifts:
        own_copy(shift).start()
        near_copy(shift).start()
    own_test = pltpu.make_async_copy(test, panels.at[0, 0], here_sem.at[0])
    own_near = pltpu.make_async_copy(near.at[0], blocks.at[0], here_sem.at[1])
    own_test.start()
    own_near.start()
    diagonal = lax.broadcasted_iota(jnp.int32, (size, size), 0) == lax.broadcasted_iota(
        jnp.int32, (size, size), 1
    )
    first = row * leaves

    def own_slot(leaf):
        slot = jnp.int32(0)
        for k in range(1, columns):
            slot = jnp.where(choice[k, leaf] == first + leaf, k, slot)
        return slot

    def own_product(leaf):
        variance = jnp.where(diagonal, nugget[pl.ds(leaf, 1), :], 0.0)
        holder = (column - leaf // piece + columns) % columns
        sample[leaf] = dot_three(
            blocks[own_slot(leaf), leaf] + variance, panels[holder, 0, leaf % piece], 1, 0
        )

    early = min(2, chunks + 1)
    share_leaves = -(-leaves // (chunks + 2 - early))
    for step in range(chunks + 2):
        if step == early:
            for shift in shifts:
                own_copy(shift).wait()
                near_copy(shift).wait()
            own_test.wait()
            own_near.wait()
        if step < chunks:
            x_copy(step).wait_recv()
            y_copy(step).start()
            for shift in shifts:
                c_copy(shift, 1, 0, step).start()
        if 1 <= step <= chunks:
            chunk = step - 1
            y_copy(chunk).wait_recv()

            @pl.when(has_out)
            def _():
                z_copy(chunk).start()

            @pl.when(jnp.logical_not(ends))
            def _():
                for shift in shifts:
                    c_copy(shift, 2, 1, chunk).start()

        if step >= 2:
            chunk = step - 2

            @pl.when(has_in)
            def _():
                z_copy(chunk).wait_recv()
                for shift in shifts:
                    c_copy(shift, 3, 1, chunk).start()

        if step >= early:
            start = (step - early) * share_leaves

            @pl.loop(start, min(start + share_leaves, leaves))
            def _(leaf):
                own_product(leaf)

    for chunk in range(chunks):
        x_copy(chunk).wait_send()
        y_copy(chunk).wait_send()
        for shift in shifts:
            c_copy(shift, 1, 0, chunk).wait()

        @pl.when(has_out)
        def _():
            z_copy(chunk).wait_send()

        @pl.when(jnp.logical_not(ends))
        def _():
            for shift in shifts:
                c_copy(shift, 2, 1, chunk).wait()

        @pl.when(has_in)
        def _():
            for shift in shifts:
                c_copy(shift, 3, 1, chunk).wait()

    corner_low = jnp.where(corner == 0, 3, jnp.where(corner == 2, 2, 1))
    corner_high = jnp.where(corner == 3, 3, jnp.where(corner == 1, 2, 1))
    grams_total = sums.at[0]
    grams_total[...] = jnp.zeros_like(grams_total)

    @pl.loop(0, leaves)
    def _(leaf):
        whole = sample[leaf]
        for other in range(1, columns):
            slot = lax.rem(own_slot(leaf) + other, columns)
            place = choice[slot, leaf] - first + leaves
            side, within = place // leaves, place % leaves
            kind = jnp.where(side == 0, corner_low, jnp.where(side == 1, 0, corner_high))
            holder = (column - within // piece + columns) % columns
            whole += dot_three(
                blocks[slot, leaf], panels[holder, kind, within % piece], 1, 0
            )
        sample[leaf] = whole
        both = dot(whole[:, :width], whole, 0, 0)
        moments[leaf] = both
        grams_total[...] += both

    share = 2 * width // columns
    side = column * share // width
    offset = pl.multiple_of(column * share % width, share)
    nodes = 2 * leaves - 1

    def climb(level):
        return pltpu.make_async_remote_copy(
            src_ref=sums.at[level], dst_ref=inbox.at[level],
            send_sem=send_up.at[level], recv_sem=recv_up.at[level],
            **peer(row=row ^ (1 << level)),
        )

    def arrive(level):
        stride = 1 << level
        climb(level).wait()
        both = sums[level] + inbox[level]
        sums[level + 1] = both
        if level + 1 < levels:
            climb(level + 1).start()

        @pl.when(row % (2 * stride) == stride)
        def _():
            load_augmented(pair, 0, both[:, :width])
            load_augmented(pair, 1, jnp.where(side == 0, inbox[level], sums[level])[:, :width])

    climb(0).start()
    for leaf in range(leaves):
        grams[leaf] = moments[leaf, :, :width]
    for node in range(leaves, nodes):
        child = 2 * (node - leaves)
        grams[node] = grams[child] + grams[child + 1]
    for node in range(nodes):
        load_augmented(work, node, grams[node])
    level = 0
    for top in range(0, width, STRIP):
        eliminate_strip(work, 0, nodes, top)
        if level < levels:
            arrive(level)
            level += 1
    while level < levels:
        arrive(level)
        level += 1

    @pl.when(row == 0)
    def _():
        load_augmented(pair, 0, sums[levels, :, :width])
        load_augmented(pair, 1, sums[levels, :, :width])

    points = pl.ds(pl.multiple_of(column * share, share), share)

    def leaf_out(leaf):
        inverse = work[leaf, :, width:]
        part_sample = sample[leaf, points, :]
        own = dot_three(inverse, part_sample[:, :width], 1, 1)
        basis[leaf] = own
        reduced = dot_three(inverse, moments[leaf, :, width:], 1, 0)
        missed[leaf] = part_sample[:, width:].T - dot_three(reduced, own, 0, 0)

    def node_out(node):
        child = 2 * (node - leaves) + side
        inner_basis[node - leaves] = dot_three(
            work[node, :, width:], work[child, pl.ds(offset, share), :width], 1, 1
        )

    jobs = [functools.partial(leaf_out, leaf) for leaf in range(leaves)]
    jobs += [functools.partial(node_out, node) for node in range(leaves, nodes)]
    strips = width // STRIP
    for at in range(strips):
        eliminate_strip(pair, 0, 2, at * STRIP)
        for job in jobs[at::strips]:
            job()
    inverse = pair[0, :, width:]
    total = sums[levels]
    if share % width:
        place_row = lax.broadcasted_iota(jnp.int32, (2 * width, share), 0)
        place_lane = lax.broadcasted_iota(jnp.int32, (2 * width, share), 1)
        chosen = jnp.where(place_row == place_lane + column * share, 1.0, 0.0)
        root = dot(total, chosen, 1, 0)
    else:
        root = jnp.where(side == 0, total[:, :width], total[:, width:])
    node = dot(inverse, pair[1, pl.ds(offset, share), :width], 1, 1)
    upper[0] = jnp.where(row == 0, dot(inverse, root, 1, 0) * scale, node)


def whole_spec():
    return pl.BlockSpec(memory_space=pltpu.VMEM)


def swept(choice, near, test, nugget, rows, columns, scale):
    leaves, size = near.shape[1], near.shape[2]
    piece, wide = test.shape[0], test.shape[2]
    width = wide // 2
    share = wide // columns
    nodes = 2 * leaves - 1
    levels = rows.bit_length() - 1
    chunks = piece * CUTS
    f32 = jnp.float32
    dma = pltpu.SemaphoreType.DMA
    smem = pl.BlockSpec(memory_space=pltpu.SMEM)
    anywhere = pl.BlockSpec(memory_space=pl.ANY)
    return pl.pallas_call(
        functools.partial(sweep_kernel, rows, columns, scale),
        in_specs=[smem, anywhere, anywhere, whole_spec()],
        out_specs=[whole_spec()] * 4,
        out_shape=[
            jax.ShapeDtypeStruct((count, width, share), f32)
            for count in (leaves, leaves, leaves - 1, 1)
        ],
        scratch_shapes=[
            pltpu.VMEM((columns, 4, piece, size, wide), f32),
            pltpu.VMEM((columns, leaves, size, size), f32),
            pltpu.VMEM((leaves, size, wide), f32),
            pltpu.VMEM((leaves, width, wide), f32),
            pltpu.VMEM((levels + 1, width, wide), f32),
            pltpu.VMEM((levels, width, wide), f32),
            pltpu.VMEM((nodes, width, width), f32),
            pltpu.VMEM((nodes, width, wide), f32),
            pltpu.VMEM((2, width, wide), f32),
        ]
        + [dma((chunks,))] * 6
        + [dma((columns - 1, 2, chunks))] * 2
        + [dma((columns - 1,))] * 4
        + [dma((levels,))] * 2
        + [dma((2,))],
        compiler_params=pltpu.CompilerParams(
            vmem_limit_bytes=LIMIT, collective_id=0, has_side_effects=True
        ),
    )(choice, near, test, nugget)


def around(block, axis):
    count = lax.axis_size(axis)
    parts = [block]
    for shift in range(1, count):
        route = [((i + shift) % count, i) for i in range(count)]
        parts.append(lax.ppermute(block, axis, route))
    return parts


def on_device(near_blocks, column_block, test_panels, nugget):
    leaves = near_blocks.shape[0]
    block = near_blocks.shape[2]
    rows = lax.axis_size("row")
    columns = lax.axis_size("col")
    choice = jnp.stack(around(column_block[:, 0], "col"))
    scale = 1.0 / math.sqrt(leaves * rows * block)
    outs = swept(
        choice, near_blocks.swapaxes(0, 1), test_panels, nugget, rows, columns, scale
    )
    return tuple(outs)


def solution(mesh):
    placed = (
        P("row", "col", None, None),
        P("row", "col"),
        P(("row", "col"), None, None),
        P("row", None),
    )
    return jax.shard_map(
        on_device,
        mesh=mesh,
        in_specs=placed,
        out_specs=(P("row", None, "col"),) * 4,
        check_vma=False,
    )
```

time: 96.4 us -> 95.3 us (0.989)
  Pallas kernels: 90.5 us -> 85.8 us
  local copies, waits for them, and re-layouts: 2.2 us -> 6.5 us
  other arithmetic: 2.04 us -> 0.66 us
    unnamed x2 -> x10, local copies, waits for them, and re-layouts: 1.22 us -> 6.5 us
    pallas_call x2 -> x1, Pallas kernels: 90.5 us -> 85.8 us  [swept(): pl.pallas_call(functools.partial(sweep_kernel, rows, columns, scale), in_...]
    select_n x2 -> x0, other arithmetic: 1.36 us -> none  [the longest x1 0.68 us: on_device(): shift = (column - within // piece + columns) % columns]
  transfers between devices with their start and end apart: 1 -> 1, of which waited for: 1 -> 1; matrix products, arithmetic and copies ran while one was open for 1% -> 0% of each run, Pallas kernels for 0% -> 0%
where the time goes in v3:
time: 95.3 us; the launch traced here: 95.1 us
  Pallas kernels  85.8 us (90%)
  local copies, waits for them, and re-layouts  6.5 us (7%)
    pallas_call x1, Pallas kernels, swept(): pl.pallas_call(functools.partial(sweep_kernel, rows, columns, scale), in_...  85.8 us
    unnamed x10, local copies, waits for them, and re-layouts  6.5 us
  transfers between devices with their start and end apart: 1, of which 1 were waited for; matrix products, arithmetic and copies ran while one was open for 0% of the time, Pallas kernels for 0%

profile of v3, /device:TPU:0, one launch (start us, length us, event | category | flops | bytes accessed | tf_op | source)
XLA Modules:
  0.0 95.1 jit_solution(4272226756891856760)
XLA Ops:
  0.6 0.5 collective-permute-start
  1.1 1.0 %collective-permute-done = s32[8]{0:T(128)S(1)} collective-permute-done((s32[8]{0:T(128)}, s32[8]{0:T(128)S(1)}, u32[]{:S(2)}, u32[]{:S(2)}) %collective-permute-start) | collective-permute-done | bytes 64 | tf_op jit(solution)/shard_map/ppermute | solution.py:457
  2.1 0.7 pad_add_fusion.choice
  2.8 0.0 copy-start
  2.8 1.6 %copy-done = f32[8,1,256,256]{3,2,1,0:T(8,128)S(1)} copy-done((f32[8,1,256,256]{3,2,1,0:T(8,128)S(1)}, f32[8,1,256,256]{3,2,1,0:T(8,128)}, u32[]{:S(2)}) %copy-start) | copy-done | bytes 2097176
  4.4 0.0 copy-start.1
  4.4 1.2 %copy-done.1 = f32[4,256,256]{2,1,0:T(8,128)S(1)} copy-done((f32[4,256,256]{2,1,0:T(8,128)S(1)}, f32[4,256,256]{2,1,0:T(8,128)}, u32[]{:S(2)}) %copy-start.1) | copy-done | bytes 1048600
  5.6 0.0 copy-start.2
  5.6 0.7 copy-done.2
  6.3 85.8 %shard_map.75 = (f32[8,128,128]{2,1,0:T(8,128)S(1)}, f32[8,128,128]{2,1,0:T(8,128)S(1)}, f32[7,128,128]{2,1,0:T(8,128)S(1)}, f32[1,128,128]{2,1,0:T(8,128)S(1)}) custom-call(s32[2,8]{1,0:T(2,128)S(1)} %pad_add_fusion.choice, f32[1,8,256,256]{3,2,1,0:T(8,128)S(1)} %bitcast.4, f32[4,256,256]{2,1,0:T(8,128)S(1)} %copy-done.1, f32[8,256]{1,0:T(8,128)S(1)} %copy-done.2), custom_call_target="tpu_custom_call" | custom-call | tf_op jit(solution)/shard_map/pallas_call | solution.py:422
  92.1 0.8 copy.12
  92.9 0.8 copy.13
  93.7 0.8 copy.14
  94.5 0.6 copy.15
Async XLA Ops:
  0.6 1.5 %collective-permute-start = (s32[8]{0:T(128)}, s32[8]{0:T(128)S(1)}, u32[]{:S(2)}, u32[]{:S(2)}) collective-permute-start(s32[8]{0:T(128)} %bitcast.5), channel_id=1, source_target_pairs={{1,0},{0,1},{3,2},{2,3},{5,4},{4,5},{7,6},{6,7},{9,8},{8,9},{11,10... | collective-permute-start | bytes 104 | tf_op jit(solution)/shard_map/ppermute | solution.py:457
  2.8 1.6 %copy-start = (f32[8,1,256,256]{3,2,1,0:T(8,128)S(1)}, f32[8,1,256,256]{3,2,1,0:T(8,128)}, u32[]{:S(2)}) copy-start(f32[8,1,256,256]{3,2,1,0:T(8,128)} %param.4) | copy-start | bytes 6291460
  4.4 1.2 %copy-start.1 = (f32[4,256,256]{2,1,0:T(8,128)S(1)}, f32[4,256,256]{2,1,0:T(8,128)}, u32[]{:S(2)}) copy-start(f32[4,256,256]{2,1,0:T(8,128)} %test.1) | copy-start | bytes 3145732
  5.6 0.7 copy-start.2

commit v4 on v3

--- a/solution.py
+++ b/solution.py
@@ -11,8 +11,8 @@
 STRIP = 32
 SLAB = 8
 CUTS = 2
-GROUP = 2
-LIMIT = 48 * 1024 * 1024
+GROUP = 4
+LIMIT = 60 * 1024 * 1024
 
 
 def dot(left, right, left_dim, right_dim):
@@ -118,6 +118,64 @@
             work[slot, below:, :] -= dot(strip[:, below:size], strip, 0, 0)
 
 
+def eliminate_packed(work, count, top):
+    size = work.shape[1]
+    below = top + STRIP
+    row = lax.broadcasted_iota(jnp.int32, (1, SLAB, size), 1)
+    lane = lax.broadcasted_iota(jnp.int32, (1, SLAB, size), 2)
+    own = pl.ds(0, count)
+    shape = (count, SLAB, size)
+    slabs = [work[own, top + at : top + at + SLAB, :] for at in range(0, STRIP, SLAB)]
+    pivots = [None] * len(slabs)
+    for step in range(STRIP):
+        at, inner = divmod(step, SLAB)
+        here = top + step
+        columns = [
+            jnp.broadcast_to(slab[:, :, here : here + 1], shape) for slab in slabs[at:]
+        ]
+        pivot = jnp.broadcast_to(columns[0][:, inner : inner + 1, :], shape)
+        inverse = 1.0 / pivot
+        pivots[at] = pivot if inner == 0 else jnp.where(row >= inner, pivot, pivots[at])
+        pivot_row = jnp.broadcast_to(slabs[at][:, inner : inner + 1, :], shape)
+        scaled = jnp.where(lane == here, 1.0, pivot_row) * inverse
+        for later in range(at, len(slabs)):
+            factor, slab = columns[later - at], slabs[later]
+            if later == at:
+                factor = jnp.where(row > inner, factor, 0.0)
+                keep = jnp.where(row > inner, 0.0, jnp.where(row == inner, 1.0, slab))
+                slab = jnp.where(lane == here, keep, slab)
+            else:
+                slab = jnp.where(lane == here, 0.0, slab)
+            slabs[later] = slab - factor * scaled
+    for at, slab in enumerate(slabs):
+        base = top + at * SLAB
+        work[own, base : base + SLAB, :] = slab * lax.rsqrt(pivots[at])
+    if below < size:
+        strip_row = lax.broadcasted_iota(jnp.int32, (STRIP, size), 0) + top
+        strip_lane = lax.broadcasted_iota(jnp.int32, (STRIP, size), 1)
+        hide = jnp.logical_and(strip_lane < below, strip_lane > strip_row)
+        rest_lane = lax.broadcasted_iota(jnp.int32, (size - below, size), 1)
+        cleared = jnp.logical_and(rest_lane >= top, rest_lane < below)
+        for slot in range(count):
+            strip = work[slot, top:below, :]
+            rest = jnp.where(cleared, 0.0, work[slot, below:, :])
+            work[slot, below:, :] = rest - dot(
+                strip[:, below:size], jnp.where(hide, 0.0, strip), 0, 0
+            )
+
+
+def inverse_of(packed):
+    row = lax.broadcasted_iota(jnp.int32, packed.shape, 0)
+    lane = lax.broadcasted_iota(jnp.int32, packed.shape, 1)
+    return jnp.where(lane <= row, packed, 0.0)
+
+
+def factor_of(packed, base):
+    row = lax.broadcasted_iota(jnp.int32, packed.shape, 0) + base
+    lane = lax.broadcasted_iota(jnp.int32, packed.shape, 1)
+    return jnp.where(lane > row, packed, jnp.where(lane == row, 1.0 / packed, 0.0))
+
+
 def peer(**place):
     return dict(device_id=place, device_id_type=pl.DeviceIdType.MESH)
 
@@ -125,7 +183,7 @@
 def sweep_kernel(
     rows, columns, scale, choice, near, test, nugget,
     basis, missed, inner_basis, upper,
-    panels, blocks, sample, moments, sums, inbox, grams, work, pair,
+    panels, blocks, sample, moments, sums, inbox, work, pair,
     send_x, recv_x, send_y, recv_y, send_z, recv_z,
     send_c, recv_c, send_own, recv_own, send_near, recv_near, send_up, recv_up, here_sem,
 ):
@@ -346,15 +404,13 @@
 
     climb(0).start()
     for leaf in range(leaves):
-        grams[leaf] = moments[leaf, :, :width]
+        work[leaf] = moments[leaf, :, :width]
     for node in range(leaves, nodes):
         child = 2 * (node - leaves)
-        grams[node] = grams[child] + grams[child + 1]
-    for node in range(nodes):
-        load_augmented(work, node, grams[node])
+        work[node] = work[child] + work[child + 1]
     level = 0
     for top in range(0, width, STRIP):
-        eliminate_strip(work, 0, nodes, top)
+        eliminate_packed(work, nodes, top)
         if level < levels:
             arrive(level)
             level += 1
@@ -370,7 +426,7 @@
     points = pl.ds(pl.multiple_of(column * share, share), share)
 
     def leaf_out(leaf):
-        inverse = work[leaf, :, width:]
+        inverse = inverse_of(work[leaf])
         part_sample = sample[leaf, points, :]
         own = dot_three(inverse, part_sample[:, :width], 1, 1)
         basis[leaf] = own
@@ -380,7 +436,8 @@
     def node_out(node):
         child = 2 * (node - leaves) + side
         inner_basis[node - leaves] = dot_three(
-            work[node, :, width:], work[child, pl.ds(offset, share), :width], 1, 1
+            inverse_of(work[node]),
+            factor_of(work[child, pl.ds(offset, share), :], offset), 1, 1,
         )
 
     jobs = [functools.partial(leaf_out, leaf) for leaf in range(leaves)]
@@ -435,7 +492,6 @@
             pltpu.VMEM((levels + 1, width, wide), f32),
             pltpu.VMEM((levels, width, wide), f32),
             pltpu.VMEM((nodes, width, width), f32),
-            pltpu.VMEM((nodes, width, wide), f32),
             pltpu.VMEM((2, width, wide), f32),
         ]
         + [dma((chunks,))] * 6

time: 95.3 us -> 90.3 us (0.948)
  Pallas kernels: 85.8 us -> 81.5 us
  local copies, waits for them, and re-layouts: 6.5 us -> 5.2 us
    pallas_call x1, Pallas kernels: 85.8 us -> 81.5 us  [swept(): pl.pallas_call(functools.partial(sweep_kernel, rows, columns, scale), in_...]
    unnamed x10 -> x8, local copies, waits for them, and re-layouts: 6.5 us -> 5.2 us
where the time goes in v4:
time: 90.3 us; the launch traced here: 90 us
  Pallas kernels  81.5 us (90%)
  local copies, waits for them, and re-layouts  5.2 us (6%)
  other arithmetic  1.22 us (1%)
  waiting for transfers between devices  0.95 us (1%)
    pallas_call x1, Pallas kernels, swept(): pl.pallas_call(functools.partial(sweep_kernel, rows, columns, scale), in_...  81.5 us
    unnamed x8, local copies, waits for them, and re-layouts  5.2 us
  transfers between devices with their start and end apart: 1, of which 1 were waited for; matrix products, arithmetic and copies ran while one was open for 0% of the time, Pallas kernels for 0%

profile of v4, /device:TPU:0, one launch (start us, length us, event | category | flops | bytes accessed | tf_op | source)
XLA Modules:
  0.0 90.0 jit_solution(18270213140651525582)
XLA Ops:
  0.6 0.5 collective-permute-start
  1.1 1.0 %collective-permute-done = s32[8]{0:T(128)S(1)} collective-permute-done((s32[8]{0:T(128)}, s32[8]{0:T(128)S(1)}, u32[]{:S(2)}, u32[]{:S(2)}) %collective-permute-start) | collective-permute-done | bytes 64 | tf_op jit(solution)/shard_map/ppermute | solution.py:513
  2.1 1.2 %pad_add_fusion.choice = s32[2,8]{1,0:T(2,128)} fusion(s32[1,8]{1,0:T(1,128)S(1)} %bitcast.7, s32[1,8]{1,0:T(1,128)} %bitcast.6), kind=kLoop, calls=%fused_computation | loop fusion | flops 16 | bytes 128 | tf_op jit(solution)/shard_map/stack | solution.py:522
  3.3 81.5 %shard_map.75 = (f32[8,128,128]{2,1,0:T(8,128)}, f32[8,128,128]{2,1,0:T(8,128)}, f32[7,128,128]{2,1,0:T(8,128)}, f32[1,128,128]{2,1,0:T(8,128)}) custom-call(s32[2,8]{1,0:T(2,128)} %pad_add_fusion.choice, f32[1,8,256,256]{3,2,1,0:T(8,128)} %bitcast.4, f32[4,256,256]{2,1,0:T(8,128)} %test.1, f32[8,256]{1,0:T(8,128)} %nugget.1), custom_call_target="tpu_custom_call" | custom-call | tf_op jit(solution)/shard_map/pallas_call | solution.py:479
  84.8 0.0 copy-start
  84.8 0.0 copy-start.1
  84.8 1.9 %copy.12 = f32[8,128,128]{2,1,0:T(8,128)} copy(f32[8,128,128]{2,1,0:T(8,128)} %get-tuple-element.8) | data formatting | bytes 1048576
  86.8 1.9 %copy.13 = f32[8,128,128]{2,1,0:T(8,128)} copy(f32[8,128,128]{2,1,0:T(8,128)} %get-tuple-element.9) | data formatting | bytes 1048576
  88.6 0.0 copy-done
  88.6 0.8 copy.14
  89.4 0.0 copy-done.1
  89.4 0.6 copy.15
Async XLA Ops:
  0.6 1.5 %collective-permute-start = (s32[8]{0:T(128)}, s32[8]{0:T(128)S(1)}, u32[]{:S(2)}, u32[]{:S(2)}) collective-permute-start(s32[8]{0:T(128)} %bitcast.5), channel_id=1, source_target_pairs={{1,0},{0,1},{3,2},{2,3},{5,4},{4,5},{7,6},{6,7},{9,8},{8,9},{11,10... | collective-permute-start | bytes 104 | tf_op jit(solution)/shard_map/ppermute | solution.py:513
  84.8 3.8 %copy-start = (f32[7,128,128]{2,1,0:T(8,128)S(1)}, f32[7,128,128]{2,1,0:T(8,128)}, u32[]{:S(2)}) copy-start(f32[7,128,128]{2,1,0:T(8,128)} %get-tuple-element.10) | copy-start | bytes 1376260
  84.8 4.6 %copy-start.1 = (f32[1,128,128]{2,1,0:T(8,128)S(1)}, f32[1,128,128]{2,1,0:T(8,128)}, u32[]{:S(2)}) copy-start(f32[1,128,128]{2,1,0:T(8,128)} %get-tuple-element.11) | copy-start | bytes 196612

commit v5 on v4

--- a/solution.py
+++ b/solution.py
@@ -185,7 +185,7 @@
     basis, missed, inner_basis, upper,
     panels, blocks, sample, moments, sums, inbox, work, pair,
     send_x, recv_x, send_y, recv_y, send_z, recv_z,
-    send_c, recv_c, send_own, recv_own, send_near, recv_near, send_up, recv_up, here_sem,
+    send_c, recv_c, send_own, recv_own, send_near, recv_near, send_up, recv_up, send_side, recv_side, here_sem,
 ):
     row, column = lax.axis_index("row"), lax.axis_index("col")
     leaves, size = near.shape[1], near.shape[2]
@@ -382,25 +382,34 @@
     offset = pl.multiple_of(column * share % width, share)
     nodes = 2 * leaves - 1
 
+    band = width // columns
+
+    def band_of(ref, level):
+        return ref.at[level, pl.ds(pl.multiple_of(column * band, band), band)]
+
     def climb(level):
         return pltpu.make_async_remote_copy(
-            src_ref=sums.at[level], dst_ref=inbox.at[level],
+            src_ref=band_of(sums, level), dst_ref=band_of(inbox, level),
             send_sem=send_up.at[level], recv_sem=recv_up.at[level],
             **peer(row=row ^ (1 << level)),
         )
 
+    def pass_on(level, shift):
+        return pltpu.make_async_remote_copy(
+            src_ref=band_of(inbox, level), dst_ref=band_of(inbox, level),
+            send_sem=send_side.at[shift - 1, level], recv_sem=recv_side.at[shift - 1, level],
+            **peer(col=(column + shift) % columns),
+        )
+
     def arrive(level):
-        stride = 1 << level
-        climb(level).wait()
-        both = sums[level] + inbox[level]
-        sums[level + 1] = both
+        climb(level).wait_recv()
         if level + 1 < levels:
+            band_of(sums, level + 1)[...] = (
+                band_of(sums, level)[...] + band_of(inbox, level)[...]
+            )
             climb(level + 1).start()
-
-        @pl.when(row % (2 * stride) == stride)
-        def _():
-            load_augmented(pair, 0, both[:, :width])
-            load_augmented(pair, 1, jnp.where(side == 0, inbox[level], sums[level])[:, :width])
+        for shift in shifts:
+            pass_on(level, shift).start()
 
     climb(0).start()
     for leaf in range(leaves):
@@ -408,21 +417,6 @@
     for node in range(leaves, nodes):
         child = 2 * (node - leaves)
         work[node] = work[child] + work[child + 1]
-    level = 0
-    for top in range(0, width, STRIP):
-        eliminate_packed(work, nodes, top)
-        if level < levels:
-            arrive(level)
-            level += 1
-    while level < levels:
-        arrive(level)
-        level += 1
-
-    @pl.when(row == 0)
-    def _():
-        load_augmented(pair, 0, sums[levels, :, :width])
-        load_augmented(pair, 1, sums[levels, :, :width])
-
     points = pl.ds(pl.multiple_of(column * share, share), share)
 
     def leaf_out(leaf):
@@ -442,11 +436,39 @@
 
     jobs = [functools.partial(leaf_out, leaf) for leaf in range(leaves)]
     jobs += [functools.partial(node_out, node) for node in range(leaves, nodes)]
-    strips = width // STRIP
-    for at in range(strips):
-        eliminate_strip(pair, 0, 2, at * STRIP)
-        for job in jobs[at::strips]:
-            job()
+    half = len(jobs) // 2
+    work_items = [
+        [functools.partial(eliminate_packed, work, nodes, top)]
+        for top in range(0, width, STRIP)
+    ] + [jobs[:half], jobs[half:]]
+    for level in range(levels):
+        low, high = (len(work_items) * at // levels for at in (level, level + 1))
+        for item in work_items[low:high]:
+            for job in item:
+                job()
+        arrive(level)
+
+    for level in range(levels):
+        for shift in shifts:
+            pass_on(level, shift).wait()
+        climb(level).wait_send()
+    for level in range(levels):
+        stride = 1 << level
+        both = sums[level] + inbox[level]
+        sums[level + 1] = both
+
+        @pl.when(row % (2 * stride) == stride)
+        def _():
+            load_augmented(pair, 0, both[:, :width])
+            load_augmented(pair, 1, jnp.where(side == 0, inbox[level], sums[level])[:, :width])
+
+    @pl.when(row == 0)
+    def _():
+        load_augmented(pair, 0, sums[levels, :, :width])
+        load_augmented(pair, 1, sums[levels, :, :width])
+
+    for top in range(0, width, STRIP):
+        eliminate_strip(pair, 0, 2, top)
     inverse = pair[0, :, width:]
     total = sums[levels]
     if share % width:
@@ -498,6 +520,7 @@
         + [dma((columns - 1, 2, chunks))] * 2
         + [dma((columns - 1,))] * 4
         + [dma((levels,))] * 2
+        + [dma((columns - 1, levels))] * 2
         + [dma((2,))],
         compiler_params=pltpu.CompilerParams(
             vmem_limit_bytes=LIMIT, collective_id=0, has_side_effects=True

time: 90.3 us -> 92.6 us (1.025)
  Pallas kernels: 81.5 us -> 83.8 us
    pallas_call x1, Pallas kernels: 81.5 us -> 83.8 us  [swept(): pl.pallas_call(functools.partial(sweep_kernel, rows, columns, scale), in_...]
where the time goes in v5:
time: 92.6 us; the launch traced here: 92.3 us
  Pallas kernels  83.8 us (90%)
  local copies, waits for them, and re-layouts  5.2 us (6%)
  other arithmetic  1.22 us (1%)
  waiting for transfers between devices  0.95 us (1%)
    pallas_call x1, Pallas kernels, swept(): pl.pallas_call(functools.partial(sweep_kernel, rows, columns, scale), in_...  83.8 us
    unnamed x8, local copies, waits for them, and re-layouts  5.2 us
  transfers between devices with their start and end apart: 1, of which 1 were waited for; matrix products, arithmetic and copies ran while one was open for 0% of the time, Pallas kernels for 0%

profile of v5, /device:TPU:0, one launch (start us, length us, event | category | flops | bytes accessed | tf_op | source)
XLA Modules:
  0.0 92.3 jit_solution(17364239270823656191)
XLA Ops:
  0.6 0.5 collective-permute-start
  1.1 1.0 %collective-permute-done = s32[8]{0:T(128)S(1)} collective-permute-done((s32[8]{0:T(128)}, s32[8]{0:T(128)S(1)}, u32[]{:S(2)}, u32[]{:S(2)}) %collective-permute-start) | collective-permute-done | bytes 64 | tf_op jit(solution)/shard_map/ppermute | solution.py:536
  2.1 1.2 %pad_add_fusion.choice = s32[2,8]{1,0:T(2,128)} fusion(s32[1,8]{1,0:T(1,128)S(1)} %bitcast.7, s32[1,8]{1,0:T(1,128)} %bitcast.6), kind=kLoop, calls=%fused_computation | loop fusion | flops 16 | bytes 128 | tf_op jit(solution)/shard_map/stack | solution.py:545
  3.3 83.8 %shard_map.75 = (f32[8,128,128]{2,1,0:T(8,128)}, f32[8,128,128]{2,1,0:T(8,128)}, f32[7,128,128]{2,1,0:T(8,128)}, f32[1,128,128]{2,1,0:T(8,128)}) custom-call(s32[2,8]{1,0:T(2,128)} %pad_add_fusion.choice, f32[1,8,256,256]{3,2,1,0:T(8,128)} %bitcast.4, f32[4,256,256]{2,1,0:T(8,128)} %test.1, f32[8,256]{1,0:T(8,128)} %nugget.1), custom_call_target="tpu_custom_call" | custom-call | tf_op jit(solution)/shard_map/pallas_call | solution.py:501
  87.1 0.0 copy-start
  87.1 0.0 copy-start.1
  87.1 1.9 %copy.12 = f32[8,128,128]{2,1,0:T(8,128)} copy(f32[8,128,128]{2,1,0:T(8,128)} %get-tuple-element.8) | data formatting | bytes 1048576
  89.1 1.9 %copy.13 = f32[8,128,128]{2,1,0:T(8,128)} copy(f32[8,128,128]{2,1,0:T(8,128)} %get-tuple-element.9) | data formatting | bytes 1048576
  90.9 0.0 copy-done
  90.9 0.8 copy.14
  91.7 0.0 copy-done.1
  91.7 0.6 copy.15
Async XLA Ops:
  0.6 1.5 %collective-permute-start = (s32[8]{0:T(128)}, s32[8]{0:T(128)S(1)}, u32[]{:S(2)}, u32[]{:S(2)}) collective-permute-start(s32[8]{0:T(128)} %bitcast.5), channel_id=1, source_target_pairs={{1,0},{0,1},{3,2},{2,3},{5,4},{4,5},{7,6},{6,7},{9,8},{8,9},{11,10... | collective-permute-start | bytes 104 | tf_op jit(solution)/shard_map/ppermute | solution.py:536
  87.1 3.8 %copy-start = (f32[7,128,128]{2,1,0:T(8,128)S(1)}, f32[7,128,128]{2,1,0:T(8,128)}, u32[]{:S(2)}) copy-start(f32[7,128,128]{2,1,0:T(8,128)} %get-tuple-element.10) | copy-start | bytes 1376260
  87.1 4.6 %copy-start.1 = (f32[1,128,128]{2,1,0:T(8,128)S(1)}, f32[1,128,128]{2,1,0:T(8,128)}, u32[]{:S(2)}) copy-start(f32[1,128,128]{2,1,0:T(8,128)} %get-tuple-element.11) | copy-start | bytes 196612
